TPU v7x, 128 devices: a whole 4x4x4 slice. The times are simulated.
128 devices in a mesh: clip: 64 (over z, y, x_hi, core), seq: 2 (over x_lo).
Axes of the slice: x: 4 (x_hi: 2, x_lo: 2; x = x_hi * 2 + x_lo), y: 4, z: 4, core: 2. Of those that a mesh axis runs over, the one named last changes fastest.
Arguments:
- query_space: bfloat16 [256, 704, 1536], P(('clip', 'seq')), may hold values from -36 to 36
- key_space: bfloat16 [256, 704, 1536], P(('clip', 'seq')), may hold values from -6 to 6
- value_space: bfloat16 [256, 704, 1536], P(('clip', 'seq')), may hold values from -6 to 6
- query_time: bfloat16 [256, 704, 1536], P(('clip', 'seq')), may hold values from -36 to 36
- key_time: bfloat16 [256, 704, 1536], P(('clip', 'seq')), may hold values from -6 to 6
- frame_counts: int32 [16], replicated, may hold values from 8 to 16, as said below
- heights: int32 [16], replicated, may hold values from 11 to 22, as said below
- widths: int32 [16], replicated, may hold values from 16 to 32, as said below
Outputs:
- time_out: bfloat16 [256, 704, 1536], P(('clip', 'seq'))
Inputs may be any that keep to these rules, and one draw needn't show every extreme that they name: The first frame_counts[c] frame slots of clip c are live; some clip has all 16. `heights`: some clip has all 22 rows. `widths`: some clip has all 32 columns.
All inputs are finite; a program needn't handle non-finite values.
Results may differ from a plain program's by a relative error of at most 0.015.
Values may be sent and summed in bfloat16 or wider, within the bound.
No kernel may reach another device: no remote copies, remote signals or barrier semaphores. Data moves between devices by JAX's collectives and lax.ppermute only.
A program may use at most 192 MiB of HBM per device.

v0:
```python
from functools import partial

import jax
import jax.numpy as jnp
from jax import lax
from jax.sharding import PartitionSpec as P

HEAD = 128
GROUP_CLIP = 4
WMAX = 32


def from_partner(value, axis, distance):
    return lax.ppermute(value, axis, [(i, i ^ 1 << distance) for i in range(lax.axis_size(axis))])


def live_slots(slots, height, width):
    return (slots // WMAX < height) & (slots % WMAX < width)


def soft_weights(scores, key_live):
    scores = jnp.where(key_live, scores, -jnp.inf)
    top = jnp.max(scores, axis=-1, keepdims=True)
    expo = jnp.exp(scores - top)
    total = jnp.sum(expo, axis=-1, keepdims=True)
    return (expo / total).astype(jnp.bfloat16)


def frame_attention(item, token_live):
    queries, keys, values, frame_live = item
    slot_count, features = queries.shape
    heads = features // HEAD
    query_heads = queries.reshape(slot_count, heads, HEAD)
    key_heads = keys.reshape(slot_count, heads, HEAD)
    value_heads = values.reshape(slot_count, heads, HEAD)
    scores = jnp.einsum(
        "phd,khd->hpk", query_heads, key_heads, preferred_element_type=jnp.float32
    ) * HEAD ** (-0.5)
    weights = soft_weights(scores, token_live[None, None, :])
    mixed = jnp.einsum("hpk,khd->phd", weights, value_heads, preferred_element_type=jnp.float32)
    keep = (token_live & frame_live)[:, None, None]
    return jnp.where(keep, mixed, 0.0).reshape(slot_count, features).astype(jnp.bfloat16)


def time_attention(queries, keys, values, frame_live, slot_live):
    frame_total, slot_count, features = queries.shape
    heads = features // HEAD
    shape = (frame_total, slot_count, heads, HEAD)
    scores = jnp.einsum(
        "fshd,gshd->shfg",
        queries.reshape(shape),
        keys.reshape(shape),
        preferred_element_type=jnp.float32,
    ) * HEAD ** (-0.5)
    weights = soft_weights(scores, frame_live[None, None, None, :])
    mixed = jnp.einsum(
        "shfg,gshd->fshd", weights, values.reshape(shape), preferred_element_type=jnp.float32
    )
    keep = (frame_live[:, None] & slot_live[None, :])[:, :, None, None]
    return (
        jnp.where(keep, mixed, 0.0).reshape(frame_total, slot_count, features).astype(jnp.bfloat16)
    )


def halve_slots(stacked, clip_pos, bit):
    side = clip_pos // (1 << bit) % 2
    half = stacked.shape[2] // 2
    kept = lax.dynamic_slice_in_dim(stacked, side * half, half, 2)
    away = lax.dynamic_slice_in_dim(stacked, (1 - side) * half, half, 2)
    arrived = from_partner(away, "clip", bit)
    lower = jnp.where(side == 0, kept, arrived)
    upper = jnp.where(side == 0, arrived, kept)
    return jnp.concatenate([lower, upper], axis=1)


def rejoin_slots(result, clip_pos, bit):
    side = clip_pos // (1 << bit) % 2
    half = result.shape[0] // 2
    kept = lax.dynamic_slice_in_dim(result, side * half, half, 0)
    away = lax.dynamic_slice_in_dim(result, (1 - side) * half, half, 0)
    arrived = from_partner(away, "clip", bit)
    lower = jnp.where(side == 0, kept, arrived)
    upper = jnp.where(side == 0, arrived, kept)
    return jnp.concatenate([lower, upper], axis=1)


def spread_frames(stacked):
    return lax.all_to_all(stacked, "seq", split_axis=2, concat_axis=1, tiled=True)


def collect_slots(result):
    return lax.all_to_all(result, "seq", split_axis=0, concat_axis=1, tiled=True)


def regroup(stacked, clip_pos, levels):
    stacked = spread_frames(stacked)
    for bit in range(levels):
        stacked = halve_slots(stacked, clip_pos, bit)
    return stacked


def restore(result, clip_pos, levels):
    for bit in reversed(range(levels)):
        result = rejoin_slots(result, clip_pos, bit)
    result = collect_slots(result)
    return result


def local(query_space, key_space, value_space, query_time, key_time, frame_counts, heights, widths):
    frame_dev, slot_count, features = query_space.shape
    seq_size = lax.axis_size("seq")
    clip_pos = lax.axis_index("clip")
    seq_pos = lax.axis_index("seq")
    levels = GROUP_CLIP.bit_length() - 1
    clip_id = clip_pos // GROUP_CLIP
    member = clip_pos % GROUP_CLIP
    picked = jnp.arange(frame_counts.shape[0], dtype=jnp.int32) == clip_id
    live_frames = jnp.sum(jnp.where(picked, frame_counts, 0))
    height = jnp.sum(jnp.where(picked, heights, 0))
    width = jnp.sum(jnp.where(picked, widths, 0))
    token_live = live_slots(jnp.arange(slot_count, dtype=jnp.int32), height, width)
    first_frame = (member * seq_size + seq_pos) * frame_dev
    local_live = first_frame + jnp.arange(frame_dev, dtype=jnp.int32) < live_frames
    space_out = lax.map(
        partial(frame_attention, token_live=token_live),
        (query_space, key_space, value_space, local_live),
    )
    moved = regroup(jnp.stack([query_time, key_time, space_out]), clip_pos, levels)
    frame_total = frame_dev * GROUP_CLIP * seq_size
    span = slot_count // (GROUP_CLIP * seq_size)
    flipped = 0
    for bit in range(levels):
        flipped = flipped + member // (1 << bit) % 2 * (1 << levels - 1 - bit)
    row_index = jnp.arange(frame_total, dtype=jnp.int32)
    block = seq_pos * GROUP_CLIP + flipped
    slot_ids = block * span + jnp.arange(span, dtype=jnp.int32)
    slot_live = live_slots(slot_ids, height, width)
    frame_live = row_index < live_frames
    result = time_attention(moved[0], moved[1], moved[2], frame_live, slot_live)
    return restore(result, clip_pos, levels)


def solution(mesh):
    return jax.shard_map(
        local,
        mesh=mesh,
        in_specs=(
            P(("clip", "seq"), None, None),
            P(("clip", "seq"), None, None),
            P(("clip", "seq"), None, None),
            P(("clip", "seq"), None, None),
            P(("clip", "seq"), None, None),
            P(),
            P(),
            P(),
        ),
        out_specs=P(("clip", "seq"), None, None),
        check_vma=False,
    )
```

profile of v0, /device:TPU:2, one launch (start us, length us, event | category | flops | bytes accessed | tf_op | source)
XLA Modules:
  0.0 701.5 jit_solution(16936277137520208240)
XLA Ops:
  0.0 1.3 select_reduce_fusion.2
  1.3 0.6 add_compare_fusion
  1.9 1.4 select_reduce_fusion
  3.3 100.6 %while.11 = (s32[]{:T(128)}, bf16[2,704,1536]{1,2,0:T(8,128)(2,1)}, pred[2]{0:T(512)(128)(4,1)S(1)}, bf16[2,704,1536]{2,1,0:T(8,128)(2,1)}, bf16[2,704,1536]{2,1...) while((s32[]{:T(128)}, bf16[2,704,1536]{1,2,0:T(8,128)(2,1)}, ...), condition=%wide.region_6.7_spmd.clone, body=%wide.region_3.6_spmd.clone.sunk | while | flops 3082923520 | bytes 91100528 | solution.py:124
  3.3 0.6 dynamic_slice.112
  3.8 2.0 fusion.61
  5.8 3.9 constant_dynamic-slice_fusion.8
  9.7 4.2 copy.84
  13.9 2.4 copy.85
  16.3 15.8 %fusion.62 = (f32[12,704]{1,0:T(8,128)S(1)}, f32[12,704,704]{1,2,0:T(8,128)}) fusion(pred[704]{0:T(1024)(128)(4,1)S(1)} %get-tuple-element.182, bf16[704,12,128]{0,2,1:T(8,128)(2,1)} %bitcast.54, bf16[704,12,128]{0,2,1:T(8,128)(2,1)} %bitcast.55), kind=kOutput, calls=%fused_computation.98.clone.1 | convolution fusion | flops 1546322560 | bytes 28149440 | tf_op jit(solution)/shard_map/while/body/eval_jaxpr/sub | solution.py:24
  32.1 1.7 constant_dynamic-slice_fusion.7
  33.8 2.4 copy.83
  36.3 12.9 %fusion.63 = bf16[704,12,128]{2,0,1:T(8,128)(2,1)} fusion(pred[704]{0:T(1024)(128)(4,1)S(1)} %get-tuple-element.181, bf16[704,12,128]{0,2,1:T(8,128)(2,1)} %bitcast.56, f32[12,704,704]{1,2,0:T(8,128)} %get-tuple-element.185, f32[12,704]{1,0:T(8,128)S(1)} %get-tuple-element.186), kind=kOutput, calls=%fused_computation.12.clone.1 | convolution fusion | flops 1536589824 | bytes 28149440 | tf_op jit(solution)/shard_map/while/body/eval_jaxpr/hpk,khd->phd/dot_general | solution.py:40
  49.1 2.8 copy.86
  51.9 1.6 constant_dynamic-update-slice_fusion.2
  53.5 0.6 dynamic_slice.112
  54.1 2.0 fusion.61
  56.1 3.9 constant_dynamic-slice_fusion.8
  60.0 4.2 copy.84
  64.1 2.4 copy.85
  66.6 15.8 %fusion.62 = (f32[12,704]{1,0:T(8,128)S(1)}, f32[12,704,704]{1,2,0:T(8,128)}) fusion(pred[704]{0:T(1024)(128)(4,1)S(1)} %get-tuple-element.182, bf16[704,12,128]{0,2,1:T(8,128)(2,1)} %bitcast.54, bf16[704,12,128]{0,2,1:T(8,128)(2,1)} %bitcast.55), kind=kOutput, calls=%fused_computation.98.clone.1 | convolution fusion | flops 1546322560 | bytes 28149440 | tf_op jit(solution)/shard_map/while/body/eval_jaxpr/sub | solution.py:24
  82.3 1.7 constant_dynamic-slice_fusion.7
  84.1 2.4 copy.83
  86.5 12.9 %fusion.63 = bf16[704,12,128]{2,0,1:T(8,128)(2,1)} fusion(pred[704]{0:T(1024)(128)(4,1)S(1)} %get-tuple-element.181, bf16[704,12,128]{0,2,1:T(8,128)(2,1)} %bitcast.56, f32[12,704,704]{1,2,0:T(8,128)} %get-tuple-element.185, f32[12,704]{1,0:T(8,128)S(1)} %get-tuple-element.186), kind=kOutput, calls=%fused_computation.12.clone.1 | convolution fusion | flops 1536589824 | bytes 28149440 | tf_op jit(solution)/shard_map/while/body/eval_jaxpr/hpk,khd->phd/dot_general | solution.py:40
  99.4 2.8 copy.86
  102.2 1.7 constant_dynamic-update-slice_fusion.2
  103.9 12.5 %copy.52 = bf16[2,704,1536]{2,0,1:T(2,128)(2,1)} copy(bf16[2,704,1536]{1,2,0:T(8,128)(2,1)} %get-tuple-element.42) | data formatting | bytes 8650752 | tf_op jit(solution)/shard_map/while | solution.py:124
  116.4 33.2 %copy_bitcast_fusion = (bf16[1,2,704,1536]{3,1,0,2:T(2,128)(2,1)S(1)}, bf16[1,2,704,1536]{3,1,0,2:T(2,128)(2,1)S(1)}) fusion(bf16[2,704,1536]{2,1,0:T(8,128)(2,1)} %param.14, bf16[2,704,1536]{2,1,0:T(8,128)(2,1)} %param.13), kind=kLoop, calls=%fused_computation.69 | loop fusion | bytes 17301504 | tf_op jit(solution)/shard_map/stack | solution.py:128
  149.6 19.6 %pad_maximum_fusion = bf16[3,2,704,1536]{3,1,0,2:T(2,128)(2,1)} fusion(bf16[1,2,704,1536]{3,1,0,2:T(2,128)(2,1)S(1)} %bitcast.60, bf16[1,2,704,1536]{3,1,0,2:T(2,128)(2,1)S(1)} %get-tuple-element.124, bf16[1,2,704,1536]{3,1,0,2:T(2,128)(2,1)S(1)} %get-tuple-element.125), kind=kLoop, calls=%fused_computation.43 | loop fusion | flops 12976128 | bytes 25952256 | tf_op jit(solution)/shard_map/stack | solution.py:128
  169.2 8.9 %all-to-all-start = ((bf16[3,2,704,1536]{3,1,0,2:T(2,128)(2,1)}), bf16[3,2,704,1536]{3,1,0,2:T(2,128)(2,1)}, u32[]{:S(2)}, u32[]{:S(2)}) async-start(bf16[3,2,704,1536]{3,1,0,2:T(2,128)(2,1)} %pad_maximum_fusion), calls=%async_computation | async-start | bytes 25952256 | tf_op jit(solution)/shard_map/all_to_all | solution.py:88
  178.1 139.3 %all-to-all-done = bf16[3,2,704,1536]{3,1,0,2:T(2,128)(2,1)} async-done(((bf16[3,2,704,1536]{3,1,0,2:T(2,128)(2,1)}), bf16[3,2,704,1536]{3,1,0,2:T(2,128)(2,1)}, u32[]{:S(2)}, u32[]{:S(2)}) %all-to-all-start) | async-done | bytes 12976160 | tf_op jit(solution)/shard_map/all_to_all | solution.py:88
  317.4 8.2 %copy.53 = bf16[3,2,704,1536]{3,2,1,0:T(8,128)(2,1)S(1)} copy(bf16[3,2,704,1536]{3,1,0,2:T(2,128)(2,1)} %all-to-all-done) | data formatting | bytes 25952256 | tf_op jit(solution)/shard_map/all_to_all | solution.py:88
  325.6 2.4 copy.54
  328.0 3.4 constant_dynamic-slice_fusion.4
  331.4 3.2 copy-done.1
  334.6 10.8 %collective-permute-done = bf16[3,4,176,1536]{3,2,1,0:T(8,128)(2,1)} collective-permute-done((bf16[3,4,176,1536]{3,2,1,0:T(8,128)(2,1)}, bf16[3,4,176,1536]{3,2,1,0:T(8,128)(2,1)}, u32[]{:S(2)}, u32[]{:S(2)}) %collective-permute-start) | collective-permute-done | bytes 6488096 | tf_op jit(solution)/shard_map/ppermute | solution.py:14
  345.4 9.1 %broadcast_select_fusion = (bf16[3,4,176,1536]{3,2,1,0:T(8,128)(2,1)S(1)}, bf16[3,4,176,1536]{3,2,1,0:T(8,128)(2,1)}) fusion(bf16[3,4,176,1536]{3,2,1,0:T(8,128)(2,1)} %collective-permute-done, pred[]{:T(512)S(6)} %eq.30, bf16[3,4,352,1536]{3,2,1,0:T(8,128)(2,1)} %bitcast.58, s32[]{:T(128)S(6)} %select_n.189), kind=kLoop, calls=%fused_computation.52 | loop fusion | flops 6488064 | bytes 25952260 | tf_op jit(solution)/shard_map/jit(_where)/select_n | solution.py:72
  354.5 7.5 %fusion.26 = bf16[3,8,88,1536]{3,2,1,0:T(8,128)(2,1)} fusion(s32[]{:T(128)S(6)} %select_n.194, bf16[3,4,176,1536]{3,2,1,0:T(8,128)(2,1)} %get-tuple-element.112, bf16[3,4,176,1536]{3,2,1,0:T(8,128)(2,1)S(1)} %get-tuple-element.111), kind=kLoop, calls=%fused_computation.50 | loop fusion | flops 12976128 | bytes 19464196 | tf_op jit(solution)/shard_map/concatenate | solution.py:73
  362.0 3.2 collective-permute-start.1
  365.2 0.6 iota_compare_fusion.1
  365.8 1.3 compare_and_fusion
  367.1 0.1 broadcast_and_fusion.1
  367.2 138.4 %collective-permute-done.1 = bf16[3,8,88,1536]{3,2,1,0:T(8,128)(2,1)} collective-permute-done((bf16[3,8,88,1536]{3,2,1,0:T(8,128)(2,1)}, bf16[3,8,88,1536]{3,2,1,0:T(8,128)(2,1)}, u32[]{:S(2)}, u32[]{:S(2)}) %collective-permute-start.1) | collective-permute-done | bytes 6488096 | tf_op jit(solution)/shard_map/ppermute | solution.py:14
  505.6 8.0 %broadcast_select_fusion.3 = (bf16[3,8,88,1536]{3,2,1,0:T(8,128)(2,1)S(1)}, bf16[3,8,88,1536]{3,2,1,0:T(8,128)(2,1)S(1)}) fusion(bf16[3,8,88,1536]{3,2,1,0:T(8,128)(2,1)} %collective-permute-done.1, pred[]{:T(512)S(6)} %eq.31, s32[]{:T(128)S(6)} %select_n.193, bf16[3,4,176,1536]{3,2,1,0:T(8,128)(2,1)} %copy-done, bf16[3,4,176,1536]{3,2,1,0:T(8,128)(2,1)} %get-tuple-element.112), kind=kLoop, calls=%fused_computation.55 | loop fusion | flops 32440320 | bytes 32440324 | tf_op jit(solution)/shard_map/jit(_where)/select_n | solution.py:71
  513.6 4.9 fusion.30
  518.5 8.8 %reshape_squeeze.10 = bf16[16,88,12,128]{3,2,1,0:T(8,128)(2,1)} reshape(bf16[1,16,88,1536]{3,2,1,0:T(8,128)(2,1)} %get-tuple-element.115) | data formatting | bytes 8650752 | tf_op jit(solution)/shard_map/reshape;squeeze | solution.py:51
  527.3 8.8 %reshape_squeeze.11 = bf16[16,88,12,128]{3,2,1,0:T(8,128)(2,1)} reshape(bf16[1,16,88,1536]{3,2,1,0:T(8,128)(2,1)} %get-tuple-element.114) | data formatting | bytes 8650752 | tf_op jit(solution)/shard_map/reshape;squeeze | solution.py:52
  536.0 9.4 %fusion.32 = f32[88,12,16,16]{2,3,1,0:T(8,128)S(1)} fusion(bf16[16,88,12,128]{3,2,1,0:T(8,128)(2,1)} %reshape_squeeze.11, bf16[16,88,12,128]{3,2,1,0:T(8,128)(2,1)} %reshape_squeeze.10), kind=kOutput, calls=%fused_computation.66 | convolution fusion | flops 69206016 | bytes 9732096 | tf_op jit(solution)/shard_map/fshd,gshd->shfg/dot_general | solution.py:49
  545.5 6.3 fusion.46
  551.8 8.8 %reshape_squeeze.9 = bf16[16,88,12,128]{3,2,1,0:T(8,128)(2,1)} reshape(bf16[1,16,88,1536]{3,2,1,0:T(8,128)(2,1)} %get-tuple-element.113) | data formatting | bytes 8650752 | tf_op jit(solution)/shard_map/reshape;squeeze | solution.py:57
  560.6 8.0 %fusion.24 = bf16[16,88,12,128]{3,0,2,1:T(8,128)(2,1)S(1)} fusion(pred[16,88]{0,1:T(8,128)(4,1)S(1)} %broadcast_and_fusion.1, f32[88,12,16,16]{2,3,1,0:T(8,128)} %get-tuple-element.121, f32[88,12,16]{2,1,0:T(8,128)S(1)} %get-tuple-element.120, bf16[16,88,12,128]{3,2,1,0:T(8,128)(2,1)} %reshape_squeeze.9), kind=kOutput, calls=%fused_computation.45 | convolution fusion | flops 74072064 | bytes 9801088 | tf_op jit(solution)/shard_map/shfg,gshd->fshd/dot_general | solution.py:56
  568.6 4.0 copy.59
  572.5 8.7 %convert_element_type.30 = bf16[16,88,1536]{2,1,0:T(8,128)(2,1)} reshape(bf16[16,88,12,128]{3,2,1,0:T(8,128)(2,1)} %copy.59) | data formatting | bytes 8650752 | tf_op jit(solution)/shard_map/convert_element_type | solution.py:61
  581.3 1.8 constant_dynamic-slice_fusion.3
  583.0 3.4 collective-permute-start.2
  586.5 46.6 %collective-permute-done.2 = bf16[8,88,1536]{2,1,0:T(8,128)(2,1)} collective-permute-done((bf16[8,88,1536]{2,1,0:T(8,128)(2,1)S(1)}, bf16[8,88,1536]{2,1,0:T(8,128)(2,1)}, u32[]{:S(2)}, u32[]{:S(2)}) %collective-permute-start.2) | collective-permute-done | bytes 2162720 | tf_op jit(solution)/shard_map/ppermute | solution.py:14
  633.1 2.5 broadcast_select_fusion.4
  635.7 1.3 copy-done.2
  637.0 1.5 fusion.39
  638.5 4.6 collective-permute-done.3
  643.1 2.9 broadcast_select_fusion.7
  646.0 0.4 pad_maximum_fusion.2
  646.4 52.6 %all_to_all.36 = bf16[4,352,1536]{2,1,0:T(8,128)(2,1)S(1)} all-to-all(bf16[4,352,1536]{2,1,0:T(8,128)(2,1)S(1)} %pad_maximum_fusion.2), channel_id=1, replica_groups=mesh['clip'=64,'seq'=2] {'seq'}, dimensions={0} | all-to-all | bytes 8650752 | tf_op jit(solution)/shard_map/all_to_all | solution.py:92
  699.0 2.3 copy.60
  (9 shorter events, 0.0 us)
Async XLA Ops:
  116.4 33.3 %copy-start.3 = (bf16[2,704,1536]{2,0,1:T(2,128)(2,1)S(1)}, bf16[2,704,1536]{2,0,1:T(2,128)(2,1)}, u32[]{:S(2)}) copy-start(bf16[2,704,1536]{2,0,1:T(2,128)(2,1)} %copy.52) | copy-start | bytes 12976132
  169.2 148.2 %all-to-all-start = ((bf16[3,2,704,1536]{3,1,0,2:T(2,128)(2,1)}), bf16[3,2,704,1536]{3,1,0,2:T(2,128)(2,1)}, u32[]{:S(2)}, u32[]{:S(2)}) async-start(bf16[3,2,704,1536]{3,1,0,2:T(2,128)(2,1)} %pad_maximum_fusion), calls=%async_computation | async-start | bytes 25952256 | tf_op jit(solution)/shard_map/all_to_all | solution.py:88
  328.0 6.6 copy-start.1
  334.6 10.8 %collective-permute-start = (bf16[3,4,176,1536]{3,2,1,0:T(8,128)(2,1)}, bf16[3,4,176,1536]{3,2,1,0:T(8,128)(2,1)}, u32[]{:S(2)}, u32[]{:S(2)}) collective-permute-start(bf16[3,4,176,1536]{3,2,1,0:T(8,128)(2,1)} %constant_dynamic-slice_fusion.4), channel_id=1, source_target_pairs={{0,2},{2,0},{4,6},{6,4},{8,10},{10,8},{12,14},{14,12},{16,18},{18,... | collective-permute-start | bytes 19464200 | tf_op jit(solution)/shard_map/ppermute | solution.py:14
  354.5 7.5 %copy-start = (bf16[3,4,176,1536]{3,2,1,0:T(8,128)(2,1)}, bf16[3,4,176,1536]{3,2,1,0:T(8,128)(2,1)S(1)}, u32[]{:S(2)}) copy-start(bf16[3,4,176,1536]{3,2,1,0:T(8,128)(2,1)S(1)} %get-tuple-element.111) | copy-start | bytes 19464196
  362.0 143.6 %collective-permute-start.1 = (bf16[3,8,88,1536]{3,2,1,0:T(8,128)(2,1)}, bf16[3,8,88,1536]{3,2,1,0:T(8,128)(2,1)}, u32[]{:S(2)}, u32[]{:S(2)}) collective-permute-start(bf16[3,8,88,1536]{3,2,1,0:T(8,128)(2,1)} %fusion.26), channel_id=1, source_target_pairs={{0,4},{2,6},{4,0},{6,2},{8,12},{10,14},{12,8},{14,10},{16,20},{18,... | collective-permute-start | bytes 19464200 | tf_op jit(solution)/shard_map/ppermute | solution.py:14
  583.0 50.0 %collective-permute-start.2 = (bf16[8,88,1536]{2,1,0:T(8,128)(2,1)S(1)}, bf16[8,88,1536]{2,1,0:T(8,128)(2,1)}, u32[]{:S(2)}, u32[]{:S(2)}) collective-permute-start(bf16[8,88,1536]{2,1,0:T(8,128)(2,1)S(1)} %constant_dynamic-slice_fusion.3), channel_id=1, source_target_pairs={{0,4},{2,6},{4,0},{6,2},{8,12},{10,14},{12,8},{14,10},{16,20},{18,... | collective-permute-start | bytes 6488072 | tf_op jit(solution)/shard_map/ppermute | solution.py:14
  635.6 1.3 copy-start.2
  638.5 4.6 collective-permute-start.3
where the time goes:
time: 712 us; the launch traced here: 702 us
  waiting for transfers between devices  340 us (48%)
  local copies, waits for them, and re-layouts  147 us (21%)
  matrix products  74.7 us (10%)
  other arithmetic  71.9 us (10%)
  blocking collectives  52.6 us (7%)
  starting transfers between devices  15.6 us (2%)
    ppermute x4, waiting for transfers between devices, from_partner(): lax.ppermute(value, axis, [(i, i ^ 1 << distance) for i in range(lax.axis...  200 us
    all_to_all x1, waiting for transfers between devices, spread_frames(): lax.all_to_all(stacked, 'seq', split_axis=2, concat_axis=1, tiled=True)  139 us
    all_to_all x1, blocking collectives, collect_slots(): lax.all_to_all(result, 'seq', split_axis=0, concat_axis=1, tiled=True)  52.6 us
    another operation x1, local copies, waits for them, and re-layouts, local(): jnp.stack([query_time, key_time, space_out])  33.2 us
    sub x2, matrix products, soft_weights(): expo = jnp.exp(scores - top)  31.5 us
    dynamic_slice x12, local copies, waits for them, and re-layouts, local(): lax.map(partial(frame_attention, token_live=token_live), (query_space, ke...  30.5 us
    dot_general x2, matrix products, frame_attention(): jnp.einsum('hpk,khd->phd', weights, value_heads, preferred_element_type=j...  25.7 us
    another operation x1, other arithmetic, local(): jnp.stack([query_time, key_time, space_out])  19.6 us
  transfers between devices with their start and end apart: 5, of which 5 were waited for; matrix products, arithmetic and copies ran while one was open for 0% of the time, Pallas kernels for 0%

commit v1 on v0

v1 whole, which is shorter than its diff:
```python
from functools import partial

import jax
import jax.numpy as jnp
from jax import lax
from jax.experimental import pallas as pl
from jax.experimental.pallas import tpu as pltpu
from jax.sharding import PartitionSpec as P

HEAD = 128
WMAX = 32
HMAX = 22
ROW = 8
CHIPS = 4
PER = 3
SIDE = 4
ROWS = SIDE * SIDE
AXES = ("clip", "seq")
SLOTS = HMAX * WMAX
FEATURES = CHIPS * PER * HEAD
GAIN = HEAD**-0.5 * 1.4426950408889634
LOW = -1e30
UNIT = 16
BLOCKS = SLOTS // UNIT
MOST = 6
SPARE = MOST * UNIT
SWEEPS = 4
ALONE = 10
REST = 20
MORE = 8
MAIN = ((0, ALONE // 2), (ALONE, REST // 2))
FURTHER = ((0, MORE // 2),)
TURNS = ((0, 2), (2, 1))
PACK = 64
REACH = 160
VMEM_LIMIT = 56 * 1024 * 1024

ME, WIDTH, COUNT, FRAMES, HEIGHT, KEPT, START = range(7)
GIVEN, GIVEN_AT, TAKEN, TAKEN_AT, HOST_AT = 8, 12, 16, 20, 24
FRAMES_OF = 32
TABLE = 128

SMEM = pl.BlockSpec(memory_space=pltpu.SMEM)
ANYWHERE = pl.BlockSpec(memory_space=pl.ANY)


def params():
    return pltpu.CompilerParams(vmem_limit_bytes=VMEM_LIMIT)


def cost(flops, megabytes, transcendentals=0):
    return pl.CostEstimate(flops=flops, bytes_accessed=megabytes * 2**20, transcendentals=transcendentals)


def half(*shape):
    return jax.ShapeDtypeStruct(shape, jnp.bfloat16)


def dot(left, right, transposed=False):
    dims = (((1,), (1 if transposed else 0,)), ((), ()))
    return lax.dot_general(left, right, dims, preferred_element_type=jnp.float32)


def lines(block):
    return pl.multiple_of(block * UNIT, UNIT)


def neighbour(row, way):
    z, y = row // SIDE, row % SIDE
    step = 1 if way % 2 == 0 else SIDE - 1
    if way < 2:
        return (z + step) % SIDE * SIDE + y
    return z * SIDE + (y + step) % SIDE


def plan_kernel(place, counts, heights, widths, table, passes, load, flow):
    me, mine = place[0] % ROW, place[0] // ROW

    def blocks(row):
        return (heights[row] * widths[row] + UNIT - 1) // UNIT

    for row in range(ROWS):
        load[row] = blocks(row)
        flow[0, row] = 0
        flow[1, row] = 0
    for sweep in range(SWEEPS):
        for axis in range(2):
            for row in range(ROWS):
                gap = load[row] - load[neighbour(row, 2 * axis)]
                share = jnp.where(gap > 0, 1, -1) * ((jnp.abs(gap) + 1) // 5)
                flow[axis, row] = jnp.clip(flow[axis, row] + share, -MOST, MOST)
        for row in range(ROWS):
            total = blocks(row)
            for axis in range(2):
                total = total - flow[axis, row] + flow[axis, neighbour(row, 2 * axis + 1)]
            load[row] = total

    def edges_of(row):
        return [
            flow[0, row],
            -flow[0, neighbour(row, 1)],
            flow[1, row],
            -flow[1, neighbour(row, 3)],
        ]

    least = jnp.int32(BLOCKS)
    for row in range(ROWS):
        least = jnp.minimum(least, blocks(row) - sum(jnp.maximum(edge, 0) for edge in edges_of(row)))

    @pl.when(least < ALONE)
    def _():
        for row in range(ROWS):
            load[row] = blocks(row)
            flow[0, row] = 0
            flow[1, row] = 0

    largest = jnp.int32(0)
    for row in range(ROWS):
        largest = jnp.maximum(largest, load[row])
    passes[0] = jnp.maximum(largest - ALONE - REST + MORE - 1, 0) // MORE

    def list_of(row):
        edges = edges_of(row)
        kept = blocks(row) - sum(jnp.maximum(edge, 0) for edge in edges)
        given = [jnp.maximum(edges[way], 0) for way in range(4)]
        taken = [jnp.maximum(-edges[way ^ 1], 0) for way in range(4)]
        given_at, taken_at = [kept], [kept]
        for way in range(3):
            given_at.append(given_at[way] + given[way])
            taken_at.append(taken_at[way] + taken[way])
        return kept, given, given_at, taken, taken_at

    kept, given, given_at, taken, taken_at = list_of(mine)
    table[ME] = me
    table[WIDTH] = widths[mine]
    table[COUNT] = heights[mine] * widths[mine]
    table[FRAMES] = counts[mine]
    table[HEIGHT] = heights[mine]
    table[KEPT] = kept
    table[START] = 0
    for way in range(4):
        table[GIVEN + way] = given[way]
        table[GIVEN_AT + way] = given_at[way]
        table[TAKEN + way] = taken[way]
        table[TAKEN_AT + way] = taken_at[way]
        table[HOST_AT + way] = list_of(neighbour(mine, way))[4][way]

    def fill(slot, carry):
        table[FRAMES_OF + slot] = counts[mine]
        return carry

    lax.fori_loop(0, BLOCKS + MOST, fill, 0)
    for way in range(4):
        giver = neighbour(mine, way ^ 1)

        def mark(slot, carry):
            table[FRAMES_OF + slot] = counts[giver]
            return carry

        lax.fori_loop(taken_at[way], taken_at[way] + taken[way], mark, 0)


def make_plan(place, counts, heights, widths):
    return pl.pallas_call(
        plan_kernel,
        in_specs=[SMEM] * 4,
        out_specs=[SMEM] * 2,
        out_shape=[jax.ShapeDtypeStruct((TABLE,), jnp.int32), jax.ShapeDtypeStruct((1,), jnp.int32)],
        scratch_shapes=[pltpu.SMEM((ROWS,), jnp.int32), pltpu.SMEM((2, ROWS), jnp.int32)],
        cost_estimate=cost(1000, 0),
        name="plan",
    )(place, counts, heights, widths)


def gather_matrix(start, width, count):
    row = lax.div(start, width)
    base = jnp.minimum(row * WMAX, SLOTS - REACH)
    at = start + lax.broadcasted_iota(jnp.int32, (PACK, REACH), 0)
    line = jnp.full((PACK, REACH), row, jnp.int32)
    for step in range(1, 5):
        line = line + jnp.where(at >= (row + step) * width, 1, 0)
    slot = at + line * (WMAX - width) - base
    slot = jnp.where(at < count, slot, -1)
    picked = lax.broadcasted_iota(jnp.int32, (PACK, REACH), 1) == slot
    return jnp.where(picked, 1.0, 0.0).astype(jnp.bfloat16)


def reach_of(start, width):
    return pl.multiple_of(jnp.minimum(lax.div(start, width) * WMAX, SLOTS - REACH), WMAX)


def chip_and_core(place):
    return (place >> 2) * 2 + (place & 1), (place >> 1) & 1


def all_of(copies):
    for copy in copies:
        copy.start()
    for copy in copies:
        copy.wait()


def pack_kernel(info, queries, keys, own, alone, *refs):
    gifts, (picks, loaded, packed, in_sems, own_sems, alone_sems, gift_sems) = refs[:4], refs[4:]
    width, count = info[WIDTH], info[COUNT]
    loads = [
        pltpu.make_async_copy((queries, keys)[i // 2].at[i % 2], loaded.at[i], in_sems.at[i]) for i in range(4)
    ]
    for copy in loads:
        copy.start()
    for index in range(SLOTS // PACK):
        picks[index] = gather_matrix(index * PACK, width, count)
    packed[:, SLOTS:, :] = jnp.zeros((4, SPARE, FEATURES), jnp.bfloat16)
    copies = []
    rows = ALONE * UNIT // 2
    for i in range(4):
        loads[i].wait()
        for index in range(SLOTS // PACK):
            window = loaded[i, pl.ds(reach_of(index * PACK, width), REACH), :]
            packed[i, pl.ds(index * PACK, PACK), :] = dot(picks[index], window).astype(jnp.bfloat16)
        mine = [pltpu.make_async_copy(packed.at[i], own.at[i], own_sems.at[i])]
        for way in range(4):
            part = packed.at[i, pl.ds(lines(info[GIVEN_AT + way]), SPARE)]
            mine.append(pltpu.make_async_copy(part, gifts[way].at[i], gift_sems.at[i, way]))
        for place in range(ROW):
            chip, core = chip_and_core(place)
            part = packed.at[i, pl.ds(core * rows, rows), pl.ds(chip * PER * HEAD, PER * HEAD)]
            mine.append(pltpu.make_async_copy(part, alone.at[place, i], alone_sems.at[i, place]))
        for copy in mine:
            copy.start()
        copies += mine
    for copy in copies:
        copy.wait()


def pack(info, queries, keys):
    own, alone, *gifts = pl.pallas_call(
        pack_kernel,
        in_specs=[SMEM, ANYWHERE, ANYWHERE],
        out_specs=[ANYWHERE] * 6,
        out_shape=[half(4, SLOTS + SPARE, FEATURES), half(ROW, 4, ALONE * UNIT // 2, PER * HEAD)]
        + [half(4, SPARE, FEATURES)] * 4,
        scratch_shapes=[
            pltpu.VMEM((SLOTS // PACK, PACK, REACH), jnp.bfloat16),
            pltpu.VMEM((4, SLOTS, FEATURES), jnp.bfloat16),
            pltpu.VMEM((4, SLOTS + SPARE, FEATURES), jnp.bfloat16),
            pltpu.SemaphoreType.DMA((4,)),
            pltpu.SemaphoreType.DMA((4,)),
            pltpu.SemaphoreType.DMA((4, ROW)),
            pltpu.SemaphoreType.DMA((4, 4)),
        ],
        compiler_params=params(),
        cost_estimate=cost(0, 40),
        name="pack",
    )(info, queries, keys)
    return own, alone, gifts


def merge_kernel(parts, info, own, *refs):
    gifts, (out, merged, own_sem, gift_sems, out_sems) = refs[:4], refs[4:]
    columns = out.shape[3]
    first = parts[0][0]
    start = info[START] + first
    size = merged.shape[1] // UNIT
    copy = pltpu.make_async_copy(own.at[:, pl.ds(lines(start), size * UNIT)], merged, own_sem)
    copy.start()
    copy.wait()

    def each(act):
        for way in range(4):
            for block in range(MOST):
                at = info[TAKEN_AT + way] + block - start

                @pl.when((block < info[TAKEN + way]) & (at >= 0) & (at < size))
                def _():
                    part = gifts[way].at[:, pl.ds(block * UNIT, UNIT)]
                    to = merged.at[:, pl.ds(lines(at), UNIT)]
                    act(pltpu.make_async_copy(part, to, gift_sems.at[way, block]))

    each(lambda copy: copy.start())
    each(lambda copy: copy.wait())
    copies = []
    for place in range(ROW):
        chip, core = chip_and_core(place)
        done = 0
        for index, (at, each_core) in enumerate(parts):
            rows = each_core * UNIT
            part = merged.at[:, pl.ds((at - first) * UNIT + core * rows, rows), pl.ds(chip * columns, columns)]
            to = out.at[place, :, pl.ds(done, rows)]
            copies.append(pltpu.make_async_copy(part, to, out_sems.at[place, index]))
            done += rows
    all_of(copies)


def merge(info, own, gifts, parts):
    count, _, features = own.shape
    rows = sum(each for _, each in parts) * UNIT
    return pl.pallas_call(
        partial(merge_kernel, parts),
        in_specs=[SMEM] + [ANYWHERE] * 5,
        out_specs=ANYWHERE,
        out_shape=half(ROW, count, rows, features // CHIPS),
        scratch_shapes=[
            pltpu.VMEM((count, 2 * rows, features), jnp.bfloat16),
            pltpu.SemaphoreType.DMA,
            pltpu.SemaphoreType.DMA((4, MOST)),
            pltpu.SemaphoreType.DMA((ROW, 2)),
        ],
        compiler_params=params(),
        cost_estimate=cost(0, max(1, 6 * count * features // FEATURES)),
        name="merge",
    )(info, own, *gifts)


QBLOCK = 176


def space_kernel(number, info, q_ref, k_ref, v_ref, own, *refs):
    gifts, (picks, qc, kc, vc, made, own_sem, gift_sems) = refs[:4], refs[4:]
    frame, which = pl.program_id(0), pl.program_id(1)
    me, width, count = info[ME], info[WIDTH], info[COUNT]
    alive = me * 2 + frame < info[FRAMES]
    column = pl.ds(pl.multiple_of(which * HEAD, HEAD), HEAD)

    @pl.when((frame == 0) & (which == 0))
    def _():
        vc[:, HEAD:] = jnp.ones((SLOTS, HEAD), jnp.bfloat16)
        made[:, SLOTS:, :] = jnp.zeros((2, SPARE, CHIPS * number * HEAD), jnp.bfloat16)
        for index in range(SLOTS // PACK):
            picks[index] = gather_matrix(index * PACK, width, count)

    @pl.when(alive)
    def _():
        for index in range(SLOTS // PACK):
            at = pl.ds(reach_of(index * PACK, width), REACH)
            to = pl.ds(index * PACK, PACK)
            window = jnp.concatenate([q_ref[0, at, :], k_ref[0, at, :], v_ref[0, at, :]], axis=1)
            found = dot(picks[index], window).astype(jnp.bfloat16)
            qc[to, :] = found[:, :HEAD]
            kc[to, :] = found[:, HEAD : 2 * HEAD]
            vc[to, :HEAD] = found[:, 2 * HEAD :]

    bias = jnp.where(lax.broadcasted_iota(jnp.int32, (1, SLOTS), 1) < count, 0.0, LOW)
    for part in range(2):
        busy = alive & (part * 2 * QBLOCK < count)

        @pl.when(busy)
        def _():
            for block in range(part * 2, part * 2 + 2):
                to = pl.ds(block * QBLOCK, QBLOCK)
                scores = dot(qc[to, :], kc[...], True) + bias
                top = jnp.max(scores, axis=-1, keepdims=True)
                expo = jnp.exp2((scores - top) * GAIN).astype(jnp.bfloat16)
                mixed = dot(expo, vc[...])
                made[frame, to, column] = (mixed[:, :HEAD] / mixed[:, HEAD:]).astype(jnp.bfloat16)

        @pl.when(jnp.logical_not(busy))
        def _():
            made[frame, pl.ds(part * 2 * QBLOCK, 2 * QBLOCK), column] = jnp.zeros((2 * QBLOCK, HEAD), jnp.bfloat16)

    @pl.when((frame == 1) & (which == CHIPS * number - 1))
    def _():
        copies = [pltpu.make_async_copy(made, own, own_sem)]
        for way in range(4):
            part = made.at[:, pl.ds(lines(info[GIVEN_AT + way]), SPARE)]
            copies.append(pltpu.make_async_copy(part, gifts[way], gift_sems.at[way]))
        all_of(copies)


def space(info, queries, keys, values, turn):
    first, number = turn
    features = CHIPS * number * HEAD
    spec = pl.BlockSpec((1, SLOTS, HEAD), lambda f, i: (f, 0, i // number * PER + first + i % number))
    steps = 2 * CHIPS * number
    own, *gifts = pl.pallas_call(
        partial(space_kernel, number),
        grid=(2, CHIPS * number),
        in_specs=[SMEM, spec, spec, spec],
        out_specs=[ANYWHERE] * 5,
        out_shape=[half(2, SLOTS + SPARE, features)] + [half(2, SPARE, features)] * 4,
        scratch_shapes=[
            pltpu.VMEM((SLOTS // PACK, PACK, REACH), jnp.bfloat16),
            pltpu.VMEM((SLOTS, HEAD), jnp.bfloat16),
            pltpu.VMEM((SLOTS, HEAD), jnp.bfloat16),
            pltpu.VMEM((SLOTS, 2 * HEAD), jnp.bfloat16),
            pltpu.VMEM((2, SLOTS + SPARE, features), jnp.bfloat16),
            pltpu.SemaphoreType.DMA,
            pltpu.SemaphoreType.DMA((4,)),
        ],
        compiler_params=params(),
        cost_estimate=cost(steps * 8 * SLOTS * SLOTS * HEAD, number * 8, steps * SLOTS * SLOTS),
        name="space",
    )(info, queries, keys, values)
    return own, gifts


def time_kernel(parts, info, *refs):
    turned, (vs, outs) = refs[: len(parts)], refs[len(parts) :]
    core = (info[ME] >> 1) & 1
    span = ROW * 2 * UNIT
    down = lax.broadcasted_iota(jnp.int32, (span, span), 0)
    along = lax.broadcasted_iota(jnp.int32, (span, span), 1)
    frame = jnp.where((down & 15) == (along & 15), along >> 4, span)
    ones = jnp.ones((span, HEAD), jnp.bfloat16)
    done = 0
    for (at, each_core), ref in zip(parts, turned):
        first = info[START] + at + core * each_core

        def step(index, carry, ref=ref, first=first, done=done):
            here = pl.ds(lines(index), UNIT)
            there = pl.ds(lines(index + done), UNIT)
            seen = frame < info[FRAMES_OF + first + index]
            queries = ref[:, 0:2, here, :].reshape(span, HEAD)
            keys = ref[:, 2:4, here, :].reshape(span, HEAD)
            values = vs[:, :, there, :].reshape(span, HEAD)
            scores = jnp.where(seen, dot(queries, keys, True), LOW)
            top = jnp.max(scores, axis=-1, keepdims=True)
            expo = jnp.exp2((scores - top) * GAIN).astype(jnp.bfloat16)
            mixed = dot(expo, jnp.concatenate([values, ones], axis=1))
            made = (mixed[:, :HEAD] / mixed[:, HEAD:]).astype(jnp.bfloat16)
            outs[:, :, there, :] = made.reshape(ROW, 2, UNIT, HEAD)
            return carry

        lax.fori_loop(0, each_core, step, 0, unroll=5 if each_core % 5 == 0 else 1)
        done += each_core


def time_attention(info, turned, values, turn, parts):
    first, number = turn
    rows = values.shape[2]
    wide = [pl.BlockSpec((ROW, 4, each * UNIT, HEAD), lambda h: (0, 0, 0, first + h)) for _, each in parts]
    thin = pl.BlockSpec((ROW, 2, rows, HEAD), lambda h: (0, 0, 0, h))
    return pl.pallas_call(
        partial(time_kernel, parts),
        grid=(number,),
        in_specs=[SMEM, *wide, thin],
        out_specs=thin,
        out_shape=half(ROW, 2, rows, number * HEAD),
        compiler_params=params(),
        cost_estimate=cost(number * rows * 16 * 256 * 128 * 4, number * 5, number * rows * 16 * 256),
        name="time",
    )(info, *turned, values)


def divide_kernel(parts, info, pieces, own, *refs):
    gifts, (merged, in_sems, own_sem, gift_sems) = refs[:4], refs[4:]
    columns = pieces.shape[3]
    size = merged.shape[1] // UNIT
    start = info[START]
    copies = []
    for place in range(ROW):
        chip, core = chip_and_core(place)
        done = 0
        for index, (at, each_core) in enumerate(parts):
            rows = each_core * UNIT
            part = merged.at[:, pl.ds(at * UNIT + core * rows, rows), pl.ds(chip * columns, columns)]
            copies.append(
                pltpu.make_async_copy(pieces.at[place, :, pl.ds(done, rows)], part, in_sems.at[place, index])
            )
            done += rows
    all_of(copies)
    copy = pltpu.make_async_copy(merged, own, own_sem)
    copy.start()

    def each(act):
        for way in range(4):
            for block in range(MOST):
                at = info[TAKEN_AT + way] + block - start

                @pl.when((block < info[TAKEN + way]) & (at >= 0) & (at < size))
                def _():
                    part = merged.at[:, pl.ds(lines(at), UNIT)]
                    to = gifts[way].at[:, pl.ds(block * UNIT, UNIT)]
                    act(pltpu.make_async_copy(part, to, gift_sems.at[way, block]))

    each(lambda copy: copy.start())
    each(lambda copy: copy.wait())
    copy.wait()


def divide(info, pieces, parts):
    features = CHIPS * pieces.shape[3]
    size = 2 * sum(each for _, each in parts)
    own, *gifts = pl.pallas_call(
        partial(divide_kernel, parts),
        in_specs=[SMEM, ANYWHERE],
        out_specs=[ANYWHERE] * 5,
        out_shape=[half(2, size * UNIT, features)] + [half(2, SPARE, features)] * 4,
        scratch_shapes=[
            pltpu.VMEM((2, size * UNIT, features), jnp.bfloat16),
            pltpu.SemaphoreType.DMA((ROW, 2)),
            pltpu.SemaphoreType.DMA,
            pltpu.SemaphoreType.DMA((4, MOST)),
        ],
        compiler_params=params(),
        cost_estimate=cost(0, max(1, 8 * features // FEATURES)),
        name="divide",
    )(info, pieces)
    return own, gifts


SPREAD = 64
SOURCE = 80


def unpack_kernel(turn, adding, info, own, *refs):
    gifts, (old, out, held, made, own_sems, gift_sems, out_sems) = refs[:4], refs[4:]
    first, number = turn
    me, width, height = info[ME], info[WIDTH], info[HEIGHT]
    start, kept = info[START], info[KEPT]
    size = own.shape[1] // UNIT

    def column(ref, frame, chip):
        return ref.at[frame, :, pl.ds((chip * PER + first) * HEAD, number * HEAD)]

    def place(frame, chip):
        return made.at[frame, :, pl.ds(chip * number * HEAD, number * HEAD)]

    spots = [(frame, chip) for frame in range(2) for chip in range(CHIPS)]
    if adding:
        all_of([pltpu.make_async_copy(column(old, *spot), place(*spot), out_sems.at[spot]) for spot in spots])
        held[...] = jnp.zeros(held.shape, jnp.bfloat16)
    else:
        copy = pltpu.make_async_copy(own, held.at[:, pl.ds(0, size * UNIT)], own_sems.at[0])
        copy.start()
        held[:, size * UNIT :, :] = jnp.zeros((2, held.shape[1] - size * UNIT, held.shape[2]), jnp.bfloat16)
        copy.wait()
        for block in range(size):

            @pl.when(block >= kept)
            def _():
                held[:, pl.ds(block * UNIT, UNIT), :] = jnp.zeros((2, UNIT, held.shape[2]), jnp.bfloat16)

    def each(act):
        if adding:
            for block in range(size):

                @pl.when(start + block < kept)
                def _():
                    part = own.at[:, pl.ds(block * UNIT, UNIT)]
                    act(pltpu.make_async_copy(part, held.at[:, pl.ds(lines(start + block), UNIT)], own_sems.at[block]))

        for way in range(4):
            for block in range(MOST):
                at = info[HOST_AT + way] + block - start

                @pl.when((block < info[GIVEN + way]) & (at >= 0) & (at < size))
                def _():
                    part = gifts[way].at[:, pl.ds(block * UNIT, UNIT)]
                    to = held.at[:, pl.ds(lines(info[GIVEN_AT + way] + block), UNIT)]
                    act(pltpu.make_async_copy(part, to, gift_sems.at[way, block]))

    each(lambda copy: copy.start())
    each(lambda copy: copy.wait())
    for index in range(SLOTS // SPREAD):
        row = index * 2
        from_row = pl.multiple_of((row * width) & -16, 16)
        at = lax.broadcasted_iota(jnp.int32, (SPREAD, SOURCE), 0)
        line = row + (at >> 5)
        wanted = line * width + (at & 31) - from_row
        wanted = jnp.where(((at & 31) < width) & (line < height), wanted, -1)
        picked = lax.broadcasted_iota(jnp.int32, (SPREAD, SOURCE), 1) == wanted
        to = pl.ds(index * SPREAD, SPREAD)
        for frame in range(2):
            alive = me * 2 + frame < info[FRAMES]
            matrix = jnp.where(picked & alive, 1.0, 0.0).astype(jnp.bfloat16)
            value = dot(matrix, held[frame, pl.ds(from_row, SOURCE), :])
            if adding:
                value = value + made[frame, to, :].astype(jnp.float32)
            made[frame, to, :] = value.astype(jnp.bfloat16)
    all_of([pltpu.make_async_copy(place(*spot), column(out, *spot), out_sems.at[spot]) for spot in spots])


def unpack(info, own, gifts, out, turn, adding):
    features = own.shape[2]
    first = out is None

    def body(info, own, *refs):
        refs = list(refs)
        if first:
            refs.insert(4, None)
        unpack_kernel(turn, adding, info, own, *refs)

    return pl.pallas_call(
        body,
        in_specs=[SMEM] + [ANYWHERE] * (5 if first else 6),
        out_specs=ANYWHERE,
        out_shape=half(2, SLOTS, FEATURES),
        input_output_aliases={} if first else {6: 0},
        scratch_shapes=[
            pltpu.VMEM((2, SLOTS + SPARE, features), jnp.bfloat16),
            pltpu.VMEM((2, SLOTS, features), jnp.bfloat16),
            pltpu.SemaphoreType.DMA((MORE,)),
            pltpu.SemaphoreType.DMA((4, MOST)),
            pltpu.SemaphoreType.DMA((2, CHIPS)),
        ],
        compiler_params=params(),
        cost_estimate=cost(0, max(1, 12 * features // FEATURES)),
        name="unpack",
    )(info, own, *gifts, *([] if first else [out]))


def step_along(value, way):
    size = lax.axis_size(AXES)
    return lax.ppermute(value, AXES, [(i, neighbour(i // ROW, way) * ROW + i % ROW) for i in range(size)])


def give(gifts):
    return [step_along(gifts[way], way) for way in range(4)]


def give_back(gifts):
    return [step_along(gifts[way], way ^ 1) for way in range(4)]


def exchange(pieces):
    size = lax.axis_size(AXES)
    groups = [list(range(i, i + ROW)) for i in range(0, size, ROW)]
    return lax.all_to_all(pieces, AXES, 0, 0, axis_index_groups=groups, tiled=True)


def after(value, *others):
    return lax.optimization_barrier((value, *others))[0]


def local(query_space, key_space, value_space, query_time, key_time, frame_counts, heights, widths):
    place = lax.axis_index(AXES).astype(jnp.int32).reshape(1)
    info, passes = make_plan(place, frame_counts, heights, widths)
    own, alone, gifts = pack(info, query_time, key_time)
    head = exchange(alone)
    gifts = give(gifts)
    spaced = []
    late = after(info, own)
    for index, turn in enumerate(TURNS):
        made, sent = space(late, query_space, key_space, value_space, turn)
        spaced.append((made, give(sent)))
        if index == 0:
            pieces = merge(info, own, after(gifts, made), MAIN[1:])
            late = after(info, pieces)
            tail = exchange(after(pieces, head))
    turned = (head, tail)
    previous = tail
    values = []
    for index, (made, sent) in enumerate(spaced):
        if index + 1 < len(spaced):
            sent = after(sent, spaced[index + 1][0])
        previous = exchange(after(merge(info, made, sent, MAIN), previous))
        values.append(previous)
    out = None
    for index, turn in enumerate(TURNS):
        made = time_attention(info, turned, values[index], turn, MAIN)
        previous = exchange(after(made, previous))
        mine, back = divide(info, previous if out is None else after(previous, out), MAIN)
        out = unpack(info, mine, give_back(back), out, turn, False)

    def further(index, out):
        here = info.at[START].set(ALONE + REST + index * MORE)
        turned = (exchange(merge(here, own, gifts, FURTHER)),)
        for (made, sent), turn in zip(spaced, TURNS):
            values = exchange(merge(here, made, sent, FURTHER))
            back = exchange(time_attention(here, turned, values, turn, FURTHER))
            mine, back = divide(here, back, FURTHER)
            out = unpack(here, mine, give_back(back), out, turn, True)
        return out

    return lax.fori_loop(0, passes[0], further, out)


def solution(mesh):
    split = P(AXES, None, None)
    return jax.shard_map(
        local,
        mesh=mesh,
        in_specs=(split,) * 5 + (P(),) * 3,
        out_specs=split,
        check_vma=False,
    )
```

time: 712 us -> 258 us (0.36); the launches traced: 702 us -> 255 us
  waiting for transfers between devices: 340 us -> 67.4 us
  local copies, waits for them, and re-layouts: 147 us -> 5.63 us
  Pallas kernels: 0 us -> 120 us
  matrix products: 74.7 us -> 0 us
  other arithmetic: 71.9 us -> 0 us
  blocking collectives: 52.6 us -> 0 us
  starting transfers between devices: 15.6 us -> 61.2 us
    ppermute x4 -> x20, waiting for transfers between devices: 200 us -> 19.9 us  [step_along(): lax.ppermute(value, AXES, [(i, neighbour(i // ROW, way) * ROW + i % ROW)...]
    pallas_call x0 -> x13, Pallas kernels: none -> 120 us  [the longest x2 65.4 us: space(): pl.pallas_call(partial(space_kernel, number), grid=(2, CHIPS * number), i...]
    all_to_all x1 -> x6, waiting for transfers between devices: 139 us -> 47.4 us  [exchange(): lax.all_to_all(pieces, AXES, 0, 0, axis_index_groups=groups, tiled=True)]
    another operation x4 -> x0, local copies, waits for them, and re-layouts: 59.6 us -> none  [the longest x1 33.2 us: local(): jnp.stack([query_time, key_time, space_out])]
    all_to_all x1 -> x0, blocking collectives: 52.6 us -> none  [collect_slots(): lax.all_to_all(result, 'seq', split_axis=0, concat_axis=1, tiled=True)]
    dot_general x4 -> x0, matrix products: 43.1 us -> none  [the longest x2 25.7 us: frame_attention(): jnp.einsum('hpk,khd->phd', weights, value_heads, preferred_element_type=j...]
    dynamic_slice x14 -> x0, local copies, waits for them, and re-layouts: 35.7 us -> none  [the longest x12 30.5 us: local(): lax.map(partial(frame_attention, token_live=token_live), (query_space, ke...]
    sub x2 -> x0, matrix products: 31.5 us -> none  [soft_weights(): expo = jnp.exp(scores - top)]
  transfers between devices with their start and end apart: 5 -> 26, of which waited for: 5 -> 11; matrix products, arithmetic and copies ran while one was open for 0% -> 0% of each run, Pallas kernels for 0% -> 39%
where the time goes in v1:
time: 258 us; the launch traced here: 255 us
  Pallas kernels  120 us (47%)
  waiting for transfers between devices  67.4 us (26%)
  starting transfers between devices  61.2 us (24%)
  local copies, waits for them, and re-layouts  5.63 us (2%)
    pallas_call x2, Pallas kernels, space(): pl.pallas_call(partial(space_kernel, number), grid=(2, CHIPS * number), i...  65.4 us
    all_to_all x6, waiting for transfers between devices, exchange(): lax.all_to_all(pieces, AXES, 0, 0, axis_index_groups=groups, tiled=True)  47.4 us
    all_to_all x6, starting transfers between devices, exchange(): lax.all_to_all(pieces, AXES, 0, 0, axis_index_groups=groups, tiled=True)  32.1 us
    ppermute x20, starting transfers between devices, step_along(): lax.ppermute(value, AXES, [(i, neighbour(i // ROW, way) * ROW + i % ROW)...  29.1 us
    ppermute x20, waiting for transfers between devices, step_along(): lax.ppermute(value, AXES, [(i, neighbour(i // ROW, way) * ROW + i % ROW)...  19.9 us
    pallas_call x3, Pallas kernels, merge(): pl.pallas_call(partial(merge_kernel, parts), in_specs=[SMEM] + [ANYWHERE]...  12 us
    pallas_call x2, Pallas kernels, time_attention(): pl.pallas_call(partial(time_kernel, parts), grid=(number,), in_specs=[SME...  11.9 us
    pallas_call x2, Pallas kernels, unpack(): pl.pallas_call(body, in_specs=[SMEM] + [ANYWHERE] * (5 if first else 6),...  10.7 us
  transfers between devices with their start and end apart: 26, of which 11 were waited for; matrix products, arithmetic and copies ran while one was open for 0% of the time, Pallas kernels for 39%

profile of v1, /device:TPU:2, one launch (start us, length us, event | category | flops | bytes accessed | tf_op | source)
XLA Modules:
  0.0 255.3 jit_solution(683233668485539467)
XLA Ops:
  0.0 3.7 %plan.1 = (s32[128]{0:T(128)S(1)}, s32[1]{0:T(128)}) custom-call(s32[1]{0:T(128)} %bitcast.1.place, s32[16]{0:T(128)} %counts.1, s32[16]{0:T(128)} %heights.1, s32[16]{0:T(128)} %widths.1), custom_call_target="tpu_custom_call" | custom-call | flops 1000 | tf_op jit(solution)/shard_map/plan/pallas_call | solution.py:164
  3.7 9.3 %pack.1 = (bf16[4,800,1536]{2,1,0:T(8,128)(2,1)}, bf16[8,4,80,384]{3,2,1,0:T(8,128)(2,1)}, bf16[4,96,1536]{2,1,0:T(8,128)(2,1)}, bf16[4,96,1536]{2,1,0:T(8,128)(...) custom-call(s32[128]{0:T(128)S(1)} %get-tuple-element.354.info, bf16[2,704,1536]{2,1,0:T(8,128)(2,1)} %queries.1, ...), custom_call_target="tpu_custom_call" | custom-call | bytes 41943040 | tf_op jit(solution)/shard_map/pack/pallas_call | solution.py:237
  13.0 4.8 %all-to-all-start.5 = ((bf16[8,4,80,384]{3,2,1,0:T(8,128)(2,1)}), bf16[8,4,80,384]{3,2,1,0:T(8,128)(2,1)}, u32[]{:S(2)}, u32[]{:S(2)}) async-start(bf16[8,4,80,384]{3,2,1,0:T(8,128)(2,1)} %get-tuple-element.341), calls=%async_computation.5 | async-start | bytes 3932160 | tf_op jit(solution)/shard_map/all_to_all | solution.py:619
  17.9 1.9 collective-permute-start.8
  19.8 2.1 collective-permute-start.9
  21.9 1.6 collective-permute-start.10
  23.5 1.7 collective-permute-start.11
  25.2 42.7 %space.2 = (bf16[2,800,1024]{2,1,0:T(8,128)(2,1)S(1)}, bf16[2,96,1024]{2,1,0:T(8,128)(2,1)}, bf16[2,96,1024]{2,1,0:T(8,128)(2,1)}, bf16[2,96,1024]{2,1,0:T(8,128)(2,1)}, bf16[2,96,1024]{2,1,0:T(8,128)(2,1)}) custom-call(s32[128]{0:T(128)S(1)} %get-tuple-element.354.info, bf16[2,704,1536]{2,1,0:T(8,128)(2,1)} %q_ref.3, bf16[2,704,1536]{2,1,0:T(8,128)(2,1)} %k_ref.3, ...), custom_call_target="tpu_custom_call" | custom-call | flops 8120172544 | bytes 16777216 | tf_op jit(solution)/shard_map/space/pallas_call | solution.py:375
  67.8 0.0 collective-permute-done.8.refs_0_
  67.9 0.0 collective-permute-done.10.refs_2_
  67.9 0.0 collective-permute-done.11.refs_3_
  67.9 1.0 copy-done
  68.9 0.3 copy-done.1
  69.2 0.4 copy-done.2
  69.7 0.4 copy-done.3
  70.0 5.5 %merge.18 = bf16[8,4,160,384]{3,2,1,0:T(8,128)(2,1)} custom-call(s32[128]{0:T(128)S(1)} %get-tuple-element.354.info, bf16[4,800,1536]{2,1,0:T(8,128)(2,1)} %get-tuple-element.563.own, bf16[4,96,1536]{2,1,0:T(8,128)(2,1)S(1)} %collective-permute-done.8.refs_0_, bf16[4,96,1536]{2,1,0:T(8,128)(2,1)S(1)} %collective-permute-done.9.refs_1_, ...), custom_call_target="tpu_custom_call" | custom-call | bytes 25165824 | tf_op jit(solution)/shard_map/merge/pallas_call | solution.py:298
  75.6 4.8 %all-to-all-start.6 = ((bf16[8,4,160,384]{3,2,1,0:T(8,128)(2,1)}), bf16[8,4,160,384]{3,2,1,0:T(8,128)(2,1)}, u32[]{:S(2)}, u32[]{:S(2)}) async-start(bf16[8,4,160,384]{3,2,1,0:T(8,128)(2,1)} %merge.18), calls=%async_computation.6 | async-start | bytes 7864320 | tf_op jit(solution)/shard_map/all_to_all | solution.py:619
  80.4 0.0 collective-permute-start.16
  80.4 3.2 %collective-permute-start.17 = (bf16[2,96,1024]{2,1,0:T(8,128)(2,1)}, bf16[2,96,1024]{2,1,0:T(8,128)(2,1)S(1)}, u32[]{:S(2)}, u32[]{:S(2)}) collective-permute-start(bf16[2,96,1024]{2,1,0:T(8,128)(2,1)} %get-tuple-element.361), channel_id=1, source_target_pairs={{0,96},{1,97},{2,98},{3,99},{4,100},{5,101},{6,102},{7,103},{8,104... | collective-permute-start | bytes 1179656 | tf_op jit(solution)/shard_map/ppermute | solution.py:605
  83.6 3.2 %collective-permute-start.19 = (bf16[2,96,1024]{2,1,0:T(8,128)(2,1)}, bf16[2,96,1024]{2,1,0:T(8,128)(2,1)S(1)}, u32[]{:S(2)}, u32[]{:S(2)}) collective-permute-start(bf16[2,96,1024]{2,1,0:T(8,128)(2,1)} %get-tuple-element.363), channel_id=1, source_target_pairs={{0,24},{1,25},{2,26},{3,27},{4,28},{5,29},{6,30},{7,31},{8,0},{9,1... | collective-permute-start | bytes 1179656 | tf_op jit(solution)/shard_map/ppermute | solution.py:605
  86.9 22.7 %space.3 = (bf16[2,800,512]{2,1,0:T(8,128)(2,1)}, bf16[2,96,512]{2,1,0:T(8,128)(2,1)}, bf16[2,96,512]{2,1,0:T(8,128)(2,1)}, bf16[2,96,512]{2,1,0:T(8,128)(2,1)}, bf16[2,96,512]{2,1,0:T(8,128)(2,1)}) custom-call(s32[128]{0:T(128)S(1)} %get-tuple-element.354.info, bf16[2,704,1536]{2,1,0:T(8,128)(2,1)} %q_ref.3, bf16[2,704,1536]{2,1,0:T(8,128)(2,1)} %k_ref.3, ...), custom_call_target="tpu_custom_call" | custom-call | flops 4060086272 | bytes 8388608 | tf_op jit(solution)/shard_map/space/pallas_call | solution.py:375
  109.6 0.0 collective-permute-done.17.refs_1_
  109.6 0.0 collective-permute-done.18.refs_2_
  109.6 0.7 copy-done.6
  110.3 0.1 copy-done.7
  110.5 0.1 copy-done.8
  110.6 0.1 copy-done.9
  110.8 3.0 %merge.20 = bf16[8,2,240,256]{3,2,1,0:T(8,128)(2,1)} custom-call(s32[128]{0:T(128)S(1)} %get-tuple-element.354.info, bf16[2,800,1024]{2,1,0:T(8,128)(2,1)S(1)} %get-tuple-element.573.own, bf16[2,96,1024]{2,1,0:T(8,128)(2,1)S(1)} %collective-permute-done.16.refs_0_, bf16[2,96,1024]{2,1,0:T(8,128)(2,1)S(1)} %collective-permute-done.17.refs_1_, ...), custom_call_target="tpu_custom_call" | custom-call | bytes 8388608 | tf_op jit(solution)/shard_map/merge/pallas_call | solution.py:298
  113.7 12.2 %all-to-all-done.6.refs_1_ = bf16[8,4,160,384]{3,2,1,0:T(8,128)(2,1)} async-done(((bf16[8,4,160,384]{3,2,1,0:T(8,128)(2,1)}), bf16[8,4,160,384]{3,2,1,0:T(8,128)(2,1)}, u32[]{:S(2)}, u32[]{:S(2)}) %all-to-all-start.6) | async-done | bytes 3932192 | tf_op jit(solution)/shard_map/all_to_all | solution.py:619
  125.9 5.7 %all-to-all-start.7 = ((bf16[8,2,240,256]{3,2,1,0:T(8,128)(2,1)}), bf16[8,2,240,256]{3,2,1,0:T(8,128)(2,1)}, u32[]{:S(2)}, u32[]{:S(2)}) async-start(bf16[8,2,240,256]{3,2,1,0:T(8,128)(2,1)} %merge.20), calls=%async_computation.7 | async-start | bytes 3932160 | tf_op jit(solution)/shard_map/all_to_all | solution.py:619
  131.6 3.2 %collective-permute-start.13 = (bf16[2,96,512]{2,1,0:T(8,128)(2,1)}, bf16[2,96,512]{2,1,0:T(8,128)(2,1)S(1)}, u32[]{:S(2)}, u32[]{:S(2)}) collective-permute-start(bf16[2,96,512]{2,1,0:T(8,128)(2,1)} %get-tuple-element.357), channel_id=1, source_target_pairs={{0,96},{1,97},{2,98},{3,99},{4,100},{5,101},{6,102},{7,103},{8,104... | collective-permute-start | bytes 589832 | tf_op jit(solution)/shard_map/ppermute | solution.py:605
  134.9 3.2 %collective-permute-start.15 = (bf16[2,96,512]{2,1,0:T(8,128)(2,1)}, bf16[2,96,512]{2,1,0:T(8,128)(2,1)S(1)}, u32[]{:S(2)}, u32[]{:S(2)}) collective-permute-start(bf16[2,96,512]{2,1,0:T(8,128)(2,1)} %get-tuple-element.359), channel_id=1, source_target_pairs={{0,24},{1,25},{2,26},{3,27},{4,28},{5,29},{6,30},{7,31},{8,0},{9,1... | collective-permute-start | bytes 589832 | tf_op jit(solution)/shard_map/ppermute | solution.py:605
  138.1 1.9 collective-permute-done.12.refs_0_
  140.0 2.7 %collective-permute-done.14.refs_2_ = bf16[2,96,512]{2,1,0:T(8,128)(2,1)S(1)} collective-permute-done((bf16[2,96,512]{2,1,0:T(8,128)(2,1)}, bf16[2,96,512]{2,1,0:T(8,128)(2,1)S(1)}, u32[]{:S(2)}, u32[]{:S(2)}) %collective-permute-start.14) | collective-permute-done | bytes 196640 | tf_op jit(solution)/shard_map/ppermute | solution.py:605
  142.7 0.7 copy-done.13
  143.4 0.7 copy-done.14
  144.0 3.5 %merge.19 = bf16[8,2,240,128]{3,2,1,0:T(8,128)(2,1)} custom-call(s32[128]{0:T(128)S(1)} %get-tuple-element.354.info, bf16[2,800,512]{2,1,0:T(8,128)(2,1)} %get-tuple-element.568.own, bf16[2,96,512]{2,1,0:T(8,128)(2,1)S(1)} %collective-permute-done.12.refs_0_, bf16[2,96,512]{2,1,0:T(8,128)(2,1)S(1)} %collective-permute-done.13.refs_1_, ...), custom_call_target="tpu_custom_call" | custom-call | bytes 4194304 | tf_op jit(solution)/shard_map/merge/pallas_call | solution.py:298
  147.5 8.6 %all-to-all-done.7.refs_2_ = bf16[8,2,240,256]{3,2,1,0:T(8,128)(2,1)} async-done(((bf16[8,2,240,256]{3,2,1,0:T(8,128)(2,1)}), bf16[8,2,240,256]{3,2,1,0:T(8,128)(2,1)}, u32[]{:S(2)}, u32[]{:S(2)}) %all-to-all-start.7) | async-done | bytes 1966112 | tf_op jit(solution)/shard_map/all_to_all | solution.py:619
  156.1 5.6 %all-to-all-start.8 = ((bf16[8,2,240,128]{3,2,1,0:T(8,128)(2,1)}), bf16[8,2,240,128]{3,2,1,0:T(8,128)(2,1)}, u32[]{:S(2)}, u32[]{:S(2)}) async-start(bf16[8,2,240,128]{3,2,1,0:T(8,128)(2,1)} %merge.19), calls=%async_computation.8 | async-start | bytes 1966080 | tf_op jit(solution)/shard_map/all_to_all | solution.py:619
  161.7 7.0 %time.13 = bf16[8,2,240,256]{3,2,1,0:T(8,128)(2,1)} custom-call(s32[128]{0:T(128)S(1)} %get-tuple-element.354.info, bf16[8,4,80,384]{3,2,1,0:T(8,128)(2,1)} %all-to-all-done.5.refs_0_, bf16[8,4,160,384]{3,2,1,0:T(8,128)(2,1)} %all-to-all-done.6.refs_1_, bf16[8,2,240,256]{3,2,1,0:T(8,128)(2,1)} %all-to-all-done.7.refs_2_), custom_call_target="tpu_custom_call" | custom-call | flops 1006632960 | bytes 10485760 | tf_op jit(solution)/shard_map/time/pallas_call | solution.py:433
  168.7 7.0 %all-to-all-done.8.refs_2_ = bf16[8,2,240,128]{3,2,1,0:T(8,128)(2,1)} async-done(((bf16[8,2,240,128]{3,2,1,0:T(8,128)(2,1)}), bf16[8,2,240,128]{3,2,1,0:T(8,128)(2,1)}, u32[]{:S(2)}, u32[]{:S(2)}) %all-to-all-start.8) | async-done | bytes 983072 | tf_op jit(solution)/shard_map/all_to_all | solution.py:619
  175.7 5.7 %all-to-all-start.9 = ((bf16[8,2,240,256]{3,2,1,0:T(8,128)(2,1)}), bf16[8,2,240,256]{3,2,1,0:T(8,128)(2,1)}, u32[]{:S(2)}, u32[]{:S(2)}) async-start(bf16[8,2,240,256]{3,2,1,0:T(8,128)(2,1)} %time.13), calls=%async_computation.9 | async-start | bytes 3932160 | tf_op jit(solution)/shard_map/all_to_all | solution.py:619
  181.4 4.9 %time.12 = bf16[8,2,240,128]{3,2,1,0:T(8,128)(2,1)} custom-call(s32[128]{0:T(128)S(1)} %get-tuple-element.354.info, bf16[8,4,80,384]{3,2,1,0:T(8,128)(2,1)} %all-to-all-done.5.refs_0_, bf16[8,4,160,384]{3,2,1,0:T(8,128)(2,1)} %all-to-all-done.6.refs_1_, bf16[8,2,240,128]{3,2,1,0:T(8,128)(2,1)} %all-to-all-done.8.refs_2_), custom_call_target="tpu_custom_call" | custom-call | flops 503316480 | bytes 5242880 | tf_op jit(solution)/shard_map/time/pallas_call | solution.py:433
  186.2 19.6 %all-to-all-done.9.pieces = bf16[8,2,240,256]{3,2,1,0:T(8,128)(2,1)} async-done(((bf16[8,2,240,256]{3,2,1,0:T(8,128)(2,1)}), bf16[8,2,240,256]{3,2,1,0:T(8,128)(2,1)}, u32[]{:S(2)}, u32[]{:S(2)}) %all-to-all-start.9) | async-done | bytes 1966112 | tf_op jit(solution)/shard_map/all_to_all | solution.py:619
  205.9 5.6 %all-to-all-start.10 = ((bf16[8,2,240,128]{3,2,1,0:T(8,128)(2,1)}), bf16[8,2,240,128]{3,2,1,0:T(8,128)(2,1)}, u32[]{:S(2)}, u32[]{:S(2)}) async-start(bf16[8,2,240,128]{3,2,1,0:T(8,128)(2,1)} %time.12), calls=%async_computation.10 | async-start | bytes 1966080 | tf_op jit(solution)/shard_map/all_to_all | solution.py:619
  211.4 3.9 %divide.12 = (bf16[2,480,1024]{2,1,0:T(8,128)(2,1)}, bf16[2,96,1024]{2,1,0:T(8,128)(2,1)}, bf16[2,96,1024]{2,1,0:T(8,128)(2,1)}, bf16[2,96,1024]{2,1,0:T(8,128)(2,1)}, bf16[2,96,1024]{2,1,0:T(8,128)(2,1)}) custom-call(s32[128]{0:T(128)S(1)} %get-tuple-element.354.info, bf16[8,2,240,256]{3,2,1,0:T(8,128)(2,1)} %all-to-all-done.9.pieces), custom_call_target="tpu_custom_call" | custom-call | bytes 5242880 | tf_op jit(solution)/shard_map/divide/pallas_call | solution.py:484
  215.3 1.9 collective-permute-start.20
  217.2 0.2 collective-permute-start.21
  217.4 2.0 collective-permute-start.23
  219.4 7.3 %collective-permute-done.20.refs_0_ = bf16[2,96,1024]{2,1,0:T(8,128)(2,1)S(1)} collective-permute-done((bf16[2,96,1024]{2,1,0:T(8,128)(2,1)}, bf16[2,96,1024]{2,1,0:T(8,128)(2,1)S(1)}, u32[]{:S(2)}, u32[]{:S(2)}) %collective-permute-start.20) | collective-permute-done | bytes 393248 | tf_op jit(solution)/shard_map/ppermute | solution.py:605
  226.8 2.7 %collective-permute-done.21.refs_1_ = bf16[2,96,1024]{2,1,0:T(8,128)(2,1)S(1)} collective-permute-done((bf16[2,96,1024]{2,1,0:T(8,128)(2,1)}, bf16[2,96,1024]{2,1,0:T(8,128)(2,1)S(1)}, u32[]{:S(2)}, u32[]{:S(2)}) %collective-permute-start.21) | collective-permute-done | bytes 393248 | tf_op jit(solution)/shard_map/ppermute | solution.py:605
  229.5 0.7 copy-done.18
  230.3 0.2 copy-done.19
  230.4 0.1 copy-done.20
  230.6 6.1 %unpack.8.refs_4_ = bf16[2,704,1536]{2,1,0:T(8,128)(2,1)} custom-call(s32[128]{0:T(128)S(1)} %get-tuple-element.354.info, bf16[2,480,1024]{2,1,0:T(8,128)(2,1)} %get-tuple-element.372.own, bf16[2,96,1024]{2,1,0:T(8,128)(2,1)} %copy-done.17, bf16[2,96,1024]{2,1,0:T(8,128)(2,1)} %copy-done.18, bf16[2,96,1024]{2,1,0:T(8,128)(2,1)} %copy-done.19, ...), custom_call_target="tpu_custom_call" | custom-call | bytes 8388608 | tf_op jit(solution)/shard_map/unpack/pallas_call | solution.py:584
  236.7 3.2 %divide.13 = (bf16[2,480,512]{2,1,0:T(8,128)(2,1)}, bf16[2,96,512]{2,1,0:T(8,128)(2,1)}, bf16[2,96,512]{2,1,0:T(8,128)(2,1)}, bf16[2,96,512]{2,1,0:T(8,128)(2,1)}, bf16[2,96,512]{2,1,0:T(8,128)(2,1)}) custom-call(s32[128]{0:T(128)S(1)} %get-tuple-element.354.info, bf16[8,2,240,128]{3,2,1,0:T(8,128)(2,1)} %all-to-all-done.10.pieces), custom_call_target="tpu_custom_call" | custom-call | bytes 2097152 | tf_op jit(solution)/shard_map/divide/pallas_call | solution.py:484
  239.9 2.7 %collective-permute-start.24 = (bf16[2,96,512]{2,1,0:T(8,128)(2,1)}, bf16[2,96,512]{2,1,0:T(8,128)(2,1)}, u32[]{:S(2)}, u32[]{:S(2)}) collective-permute-start(bf16[2,96,512]{2,1,0:T(8,128)(2,1)} %get-tuple-element.379), channel_id=1, source_target_pairs={{0,96},{1,97},{2,98},{3,99},{4,100},{5,101},{6,102},{7,103},{8,104... | collective-permute-start | bytes 589832 | tf_op jit(solution)/shard_map/ppermute | solution.py:605
  242.6 0.1 collective-permute-start.26
  242.7 1.9 collective-permute-start.27
  244.6 1.5 collective-permute-done.24.refs_0_
  246.1 3.7 %collective-permute-done.25.refs_1_ = bf16[2,96,512]{2,1,0:T(8,128)(2,1)} collective-permute-done((bf16[2,96,512]{2,1,0:T(8,128)(2,1)}, bf16[2,96,512]{2,1,0:T(8,128)(2,1)}, u32[]{:S(2)}, u32[]{:S(2)}) %collective-permute-start.25) | collective-permute-done | bytes 196640 | tf_op jit(solution)/shard_map/ppermute | solution.py:605
  249.8 0.1 collective-permute-done.27.refs_3_
  249.9 4.6 %unpack.9 = bf16[2,704,1536]{2,1,0:T(8,128)(2,1)} custom-call(s32[128]{0:T(128)S(1)} %get-tuple-element.354.info, bf16[2,480,512]{2,1,0:T(8,128)(2,1)} %get-tuple-element.378.own, bf16[2,96,512]{2,1,0:T(8,128)(2,1)} %collective-permute-done.24.refs_0_, bf16[2,96,512]{2,1,0:T(8,128)(2,1)} %collective-permute-done.25.refs_1_, ...), custom_call_target="tpu_custom_call", output_to_operand_aliasing={{}: (6, {})} | custom-call | bytes 4194304 | tf_op jit(solution)/shard_map/unpack/pallas_call | solution.py:584
  254.5 0.6 while.14
  (32 shorter events, 0.1 us)
Async XLA Ops:
  13.0 62.5 %all-to-all-start.5 = ((bf16[8,4,80,384]{3,2,1,0:T(8,128)(2,1)}), bf16[8,4,80,384]{3,2,1,0:T(8,128)(2,1)}, u32[]{:S(2)}, u32[]{:S(2)}) async-start(bf16[8,4,80,384]{3,2,1,0:T(8,128)(2,1)} %get-tuple-element.341), calls=%async_computation.5 | async-start | bytes 3932160 | tf_op jit(solution)/shard_map/all_to_all | solution.py:619
  17.9 50.0 %collective-permute-start.8 = (bf16[4,96,1536]{2,1,0:T(8,128)(2,1)}, bf16[4,96,1536]{2,1,0:T(8,128)(2,1)S(1)}, u32[]{:S(2)}, u32[]{:S(2)}) collective-permute-start(bf16[4,96,1536]{2,1,0:T(8,128)(2,1)} %get-tuple-element.343), channel_id=1, source_target_pairs={{0,32},{1,33},{2,34},{3,35},{4,36},{5,37},{6,38},{7,39},{8,40},{9,... | collective-permute-start | bytes 3538952 | tf_op jit(solution)/shard_map/ppermute | solution.py:605
  19.8 48.1 %collective-permute-start.9 = (bf16[4,96,1536]{2,1,0:T(8,128)(2,1)}, bf16[4,96,1536]{2,1,0:T(8,128)(2,1)S(1)}, u32[]{:S(2)}, u32[]{:S(2)}) collective-permute-start(bf16[4,96,1536]{2,1,0:T(8,128)(2,1)} %get-tuple-element.344), channel_id=1, source_target_pairs={{0,96},{1,97},{2,98},{3,99},{4,100},{5,101},{6,102},{7,103},{8,104... | collective-permute-start | bytes 3538952 | tf_op jit(solution)/shard_map/ppermute | solution.py:605
  21.9 46.0 %collective-permute-start.10 = (bf16[4,96,1536]{2,1,0:T(8,128)(2,1)}, bf16[4,96,1536]{2,1,0:T(8,128)(2,1)S(1)}, u32[]{:S(2)}, u32[]{:S(2)}) collective-permute-start(bf16[4,96,1536]{2,1,0:T(8,128)(2,1)} %get-tuple-element.345), channel_id=1, source_target_pairs={{0,8},{1,9},{2,10},{3,11},{4,12},{5,13},{6,14},{7,15},{8,16},{9,17... | collective-permute-start | bytes 3538952 | tf_op jit(solution)/shard_map/ppermute | solution.py:605
  23.5 44.4 %collective-permute-start.11 = (bf16[4,96,1536]{2,1,0:T(8,128)(2,1)}, bf16[4,96,1536]{2,1,0:T(8,128)(2,1)S(1)}, u32[]{:S(2)}, u32[]{:S(2)}) collective-permute-start(bf16[4,96,1536]{2,1,0:T(8,128)(2,1)} %get-tuple-element.346), channel_id=1, source_target_pairs={{0,24},{1,25},{2,26},{3,27},{4,28},{5,29},{6,30},{7,31},{8,0},{9,1... | collective-permute-start | bytes 3538952 | tf_op jit(solution)/shard_map/ppermute | solution.py:605
  67.9 1.0 copy-start
  67.9 1.4 copy-start.1
  67.9 1.8 copy-start.2
  67.9 2.1 copy-start.3
  75.6 50.4 %all-to-all-start.6 = ((bf16[8,4,160,384]{3,2,1,0:T(8,128)(2,1)}), bf16[8,4,160,384]{3,2,1,0:T(8,128)(2,1)}, u32[]{:S(2)}, u32[]{:S(2)}) async-start(bf16[8,4,160,384]{3,2,1,0:T(8,128)(2,1)} %merge.18), calls=%async_computation.6 | async-start | bytes 7864320 | tf_op jit(solution)/shard_map/all_to_all | solution.py:619
  80.4 29.2 %collective-permute-start.16 = (bf16[2,96,1024]{2,1,0:T(8,128)(2,1)}, bf16[2,96,1024]{2,1,0:T(8,128)(2,1)S(1)}, u32[]{:S(2)}, u32[]{:S(2)}) collective-permute-start(bf16[2,96,1024]{2,1,0:T(8,128)(2,1)} %get-tuple-element.360), channel_id=1, source_target_pairs={{0,32},{1,33},{2,34},{3,35},{4,36},{5,37},{6,38},{7,39},{8,40},{9,... | collective-permute-start | bytes 1179656 | tf_op jit(solution)/shard_map/ppermute | solution.py:605
  80.4 29.2 %collective-permute-start.17 = (bf16[2,96,1024]{2,1,0:T(8,128)(2,1)}, bf16[2,96,1024]{2,1,0:T(8,128)(2,1)S(1)}, u32[]{:S(2)}, u32[]{:S(2)}) collective-permute-start(bf16[2,96,1024]{2,1,0:T(8,128)(2,1)} %get-tuple-element.361), channel_id=1, source_target_pairs={{0,96},{1,97},{2,98},{3,99},{4,100},{5,101},{6,102},{7,103},{8,104... | collective-permute-start | bytes 1179656 | tf_op jit(solution)/shard_map/ppermute | solution.py:605
  83.6 26.0 %collective-permute-start.18 = (bf16[2,96,1024]{2,1,0:T(8,128)(2,1)}, bf16[2,96,1024]{2,1,0:T(8,128)(2,1)S(1)}, u32[]{:S(2)}, u32[]{:S(2)}) collective-permute-start(bf16[2,96,1024]{2,1,0:T(8,128)(2,1)} %get-tuple-element.362), channel_id=1, source_target_pairs={{0,8},{1,9},{2,10},{3,11},{4,12},{5,13},{6,14},{7,15},{8,16},{9,17... | collective-permute-start | bytes 1179656 | tf_op jit(solution)/shard_map/ppermute | solution.py:605
  83.6 26.0 %collective-permute-start.19 = (bf16[2,96,1024]{2,1,0:T(8,128)(2,1)}, bf16[2,96,1024]{2,1,0:T(8,128)(2,1)S(1)}, u32[]{:S(2)}, u32[]{:S(2)}) collective-permute-start(bf16[2,96,1024]{2,1,0:T(8,128)(2,1)} %get-tuple-element.363), channel_id=1, source_target_pairs={{0,24},{1,25},{2,26},{3,27},{4,28},{5,29},{6,30},{7,31},{8,0},{9,1... | collective-permute-start | bytes 1179656 | tf_op jit(solution)/shard_map/ppermute | solution.py:605
  109.6 0.7 copy-start.6
  109.6 0.9 copy-start.7
  109.6 1.0 copy-start.8
  109.6 1.1 copy-start.9
  125.9 30.2 %all-to-all-start.7 = ((bf16[8,2,240,256]{3,2,1,0:T(8,128)(2,1)}), bf16[8,2,240,256]{3,2,1,0:T(8,128)(2,1)}, u32[]{:S(2)}, u32[]{:S(2)}) async-start(bf16[8,2,240,256]{3,2,1,0:T(8,128)(2,1)} %merge.20), calls=%async_computation.7 | async-start | bytes 3932160 | tf_op jit(solution)/shard_map/all_to_all | solution.py:619
  131.6 8.4 %collective-permute-start.12 = (bf16[2,96,512]{2,1,0:T(8,128)(2,1)}, bf16[2,96,512]{2,1,0:T(8,128)(2,1)S(1)}, u32[]{:S(2)}, u32[]{:S(2)}) collective-permute-start(bf16[2,96,512]{2,1,0:T(8,128)(2,1)} %get-tuple-element.356), channel_id=1, source_target_pairs={{0,32},{1,33},{2,34},{3,35},{4,36},{5,37},{6,38},{7,39},{8,40},{9,... | collective-permute-start | bytes 589832 | tf_op jit(solution)/shard_map/ppermute | solution.py:605
  131.6 8.4 %collective-permute-start.13 = (bf16[2,96,512]{2,1,0:T(8,128)(2,1)}, bf16[2,96,512]{2,1,0:T(8,128)(2,1)S(1)}, u32[]{:S(2)}, u32[]{:S(2)}) collective-permute-start(bf16[2,96,512]{2,1,0:T(8,128)(2,1)} %get-tuple-element.357), channel_id=1, source_target_pairs={{0,96},{1,97},{2,98},{3,99},{4,100},{5,101},{6,102},{7,103},{8,104... | collective-permute-start | bytes 589832 | tf_op jit(solution)/shard_map/ppermute | solution.py:605
  134.9 7.8 %collective-permute-start.14 = (bf16[2,96,512]{2,1,0:T(8,128)(2,1)}, bf16[2,96,512]{2,1,0:T(8,128)(2,1)S(1)}, u32[]{:S(2)}, u32[]{:S(2)}) collective-permute-start(bf16[2,96,512]{2,1,0:T(8,128)(2,1)} %get-tuple-element.358), channel_id=1, source_target_pairs={{0,8},{1,9},{2,10},{3,11},{4,12},{5,13},{6,14},{7,15},{8,16},{9,17... | collective-permute-start | bytes 589832 | tf_op jit(solution)/shard_map/ppermute | solution.py:605
  134.9 7.8 %collective-permute-start.15 = (bf16[2,96,512]{2,1,0:T(8,128)(2,1)}, bf16[2,96,512]{2,1,0:T(8,128)(2,1)S(1)}, u32[]{:S(2)}, u32[]{:S(2)}) collective-permute-start(bf16[2,96,512]{2,1,0:T(8,128)(2,1)} %get-tuple-element.359), channel_id=1, source_target_pairs={{0,24},{1,25},{2,26},{3,27},{4,28},{5,29},{6,30},{7,31},{8,0},{9,1... | collective-permute-start | bytes 589832 | tf_op jit(solution)/shard_map/ppermute | solution.py:605
  140.0 2.7 %copy-start.12 = (bf16[2,96,512]{2,1,0:T(8,128)(2,1)}, bf16[2,96,512]{2,1,0:T(8,128)(2,1)S(1)}, u32[]{:S(2)}) copy-start(bf16[2,96,512]{2,1,0:T(8,128)(2,1)S(1)} %collective-permute-done.13.refs_1_) | copy-start | bytes 589828
  142.7 0.7 copy-start.13
  143.4 0.7 copy-start.14
  156.1 19.5 %all-to-all-start.8 = ((bf16[8,2,240,128]{3,2,1,0:T(8,128)(2,1)}), bf16[8,2,240,128]{3,2,1,0:T(8,128)(2,1)}, u32[]{:S(2)}, u32[]{:S(2)}) async-start(bf16[8,2,240,128]{3,2,1,0:T(8,128)(2,1)} %merge.19), calls=%async_computation.8 | async-start | bytes 1966080 | tf_op jit(solution)/shard_map/all_to_all | solution.py:619
  175.7 30.2 %all-to-all-start.9 = ((bf16[8,2,240,256]{3,2,1,0:T(8,128)(2,1)}), bf16[8,2,240,256]{3,2,1,0:T(8,128)(2,1)}, u32[]{:S(2)}, u32[]{:S(2)}) async-start(bf16[8,2,240,256]{3,2,1,0:T(8,128)(2,1)} %time.13), calls=%async_computation.9 | async-start | bytes 3932160 | tf_op jit(solution)/shard_map/all_to_all | solution.py:619
  205.9 30.8 %all-to-all-start.10 = ((bf16[8,2,240,128]{3,2,1,0:T(8,128)(2,1)}), bf16[8,2,240,128]{3,2,1,0:T(8,128)(2,1)}, u32[]{:S(2)}, u32[]{:S(2)}) async-start(bf16[8,2,240,128]{3,2,1,0:T(8,128)(2,1)} %time.12), calls=%async_computation.10 | async-start | bytes 1966080 | tf_op jit(solution)/shard_map/all_to_all | solution.py:619
  215.3 11.4 %collective-permute-start.20 = (bf16[2,96,1024]{2,1,0:T(8,128)(2,1)}, bf16[2,96,1024]{2,1,0:T(8,128)(2,1)S(1)}, u32[]{:S(2)}, u32[]{:S(2)}) collective-permute-start(bf16[2,96,1024]{2,1,0:T(8,128)(2,1)} %get-tuple-element.373), channel_id=1, source_target_pairs={{0,96},{1,97},{2,98},{3,99},{4,100},{5,101},{6,102},{7,103},{8,104... | collective-permute-start | bytes 1179656 | tf_op jit(solution)/shard_map/ppermute | solution.py:605
  217.2 12.3 %collective-permute-start.21 = (bf16[2,96,1024]{2,1,0:T(8,128)(2,1)}, bf16[2,96,1024]{2,1,0:T(8,128)(2,1)S(1)}, u32[]{:S(2)}, u32[]{:S(2)}) collective-permute-start(bf16[2,96,1024]{2,1,0:T(8,128)(2,1)} %get-tuple-element.374), channel_id=1, source_target_pairs={{0,32},{1,33},{2,34},{3,35},{4,36},{5,37},{6,38},{7,39},{8,40},{9,... | collective-permute-start | bytes 1179656 | tf_op jit(solution)/shard_map/ppermute | solution.py:605
  217.4 12.1 %collective-permute-start.22 = (bf16[2,96,1024]{2,1,0:T(8,128)(2,1)}, bf16[2,96,1024]{2,1,0:T(8,128)(2,1)S(1)}, u32[]{:S(2)}, u32[]{:S(2)}) collective-permute-start(bf16[2,96,1024]{2,1,0:T(8,128)(2,1)} %get-tuple-element.375), channel_id=1, source_target_pairs={{0,24},{1,25},{2,26},{3,27},{4,28},{5,29},{6,30},{7,31},{8,0},{9,1... | collective-permute-start | bytes 1179656 | tf_op jit(solution)/shard_map/ppermute | solution.py:605
  217.4 12.1 %collective-permute-start.23 = (bf16[2,96,1024]{2,1,0:T(8,128)(2,1)}, bf16[2,96,1024]{2,1,0:T(8,128)(2,1)S(1)}, u32[]{:S(2)}, u32[]{:S(2)}) collective-permute-start(bf16[2,96,1024]{2,1,0:T(8,128)(2,1)} %get-tuple-element.376), channel_id=1, source_target_pairs={{0,8},{1,9},{2,10},{3,11},{4,12},{5,13},{6,14},{7,15},{8,16},{9,17... | collective-permute-start | bytes 1179656 | tf_op jit(solution)/shard_map/ppermute | solution.py:605
  226.8 2.7 %copy-start.17 = (bf16[2,96,1024]{2,1,0:T(8,128)(2,1)}, bf16[2,96,1024]{2,1,0:T(8,128)(2,1)S(1)}, u32[]{:S(2)}) copy-start(bf16[2,96,1024]{2,1,0:T(8,128)(2,1)S(1)} %collective-permute-done.20.refs_0_) | copy-start | bytes 1179652
  229.5 0.8 copy-start.18
  229.5 1.0 copy-start.19
  229.5 1.1 copy-start.20
  239.9 6.2 %collective-permute-start.24 = (bf16[2,96,512]{2,1,0:T(8,128)(2,1)}, bf16[2,96,512]{2,1,0:T(8,128)(2,1)}, u32[]{:S(2)}, u32[]{:S(2)}) collective-permute-start(bf16[2,96,512]{2,1,0:T(8,128)(2,1)} %get-tuple-element.379), channel_id=1, source_target_pairs={{0,96},{1,97},{2,98},{3,99},{4,100},{5,101},{6,102},{7,103},{8,104... | collective-permute-start | bytes 589832 | tf_op jit(solution)/shard_map/ppermute | solution.py:605
  242.6 7.2 %collective-permute-start.25 = (bf16[2,96,512]{2,1,0:T(8,128)(2,1)}, bf16[2,96,512]{2,1,0:T(8,128)(2,1)}, u32[]{:S(2)}, u32[]{:S(2)}) collective-permute-start(bf16[2,96,512]{2,1,0:T(8,128)(2,1)} %get-tuple-element.380), channel_id=1, source_target_pairs={{0,32},{1,33},{2,34},{3,35},{4,36},{5,37},{6,38},{7,39},{8,40},{9,... | collective-permute-start | bytes 589832 | tf_op jit(solution)/shard_map/ppermute | solution.py:605
  242.6 7.2 %collective-permute-start.26 = (bf16[2,96,512]{2,1,0:T(8,128)(2,1)}, bf16[2,96,512]{2,1,0:T(8,128)(2,1)}, u32[]{:S(2)}, u32[]{:S(2)}) collective-permute-start(bf16[2,96,512]{2,1,0:T(8,128)(2,1)} %get-tuple-element.381), channel_id=1, source_target_pairs={{0,24},{1,25},{2,26},{3,27},{4,28},{5,29},{6,30},{7,31},{8,0},{9,1... | collective-permute-start | bytes 589832 | tf_op jit(solution)/shard_map/ppermute | solution.py:605
  242.7 7.2 %collective-permute-start.27 = (bf16[2,96,512]{2,1,0:T(8,128)(2,1)}, bf16[2,96,512]{2,1,0:T(8,128)(2,1)}, u32[]{:S(2)}, u32[]{:S(2)}) collective-permute-start(bf16[2,96,512]{2,1,0:T(8,128)(2,1)} %get-tuple-element.382), channel_id=1, source_target_pairs={{0,8},{1,9},{2,10},{3,11},{4,12},{5,13},{6,14},{7,15},{8,16},{9,17... | collective-permute-start | bytes 589832 | tf_op jit(solution)/shard_map/ppermute | solution.py:605

commit v2 on v1

--- a/solution.py
+++ b/solution.py
@@ -24,13 +24,13 @@
 BLOCKS = SLOTS // UNIT
 MOST = 6
 SPARE = MOST * UNIT
-SWEEPS = 4
+DIVISORS = (4, 2, 2)
 ALONE = 10
 REST = 20
 MORE = 8
 MAIN = ((0, ALONE // 2), (ALONE, REST // 2))
 FURTHER = ((0, MORE // 2),)
-TURNS = ((0, 2), (2, 1))
+TURNS = ((0, 1), (1, 2))
 PACK = 64
 REACH = 160
 VMEM_LIMIT = 56 * 1024 * 1024
@@ -83,17 +83,17 @@
         load[row] = blocks(row)
         flow[0, row] = 0
         flow[1, row] = 0
-    for sweep in range(SWEEPS):
+    for divisor in DIVISORS:
         for axis in range(2):
             for row in range(ROWS):
-                gap = load[row] - load[neighbour(row, 2 * axis)]
-                share = jnp.where(gap > 0, 1, -1) * ((jnp.abs(gap) + 1) // 5)
-                flow[axis, row] = jnp.clip(flow[axis, row] + share, -MOST, MOST)
-        for row in range(ROWS):
-            total = blocks(row)
-            for axis in range(2):
-                total = total - flow[axis, row] + flow[axis, neighbour(row, 2 * axis + 1)]
-            load[row] = total
+                other = neighbour(row, 2 * axis)
+                gap = load[row] - load[other]
+                share = jnp.where(gap > 0, 1, -1) * lax.div(jnp.abs(gap), divisor)
+                old = flow[axis, row]
+                new = jnp.clip(old + share, -MOST, MOST)
+                flow[axis, row] = new
+                load[row] = load[row] - (new - old)
+                load[other] = load[other] + (new - old)
 
     def edges_of(row):
         return [
@@ -312,7 +312,7 @@
     )(info, own, *gifts)
 
 
-QBLOCK = 176
+QBLOCK = SLOTS // 2
 
 
 def space_kernel(number, info, q_ref, k_ref, v_ref, own, *refs):
@@ -341,22 +341,32 @@
             vc[to, :HEAD] = found[:, 2 * HEAD :]
 
     bias = jnp.where(lax.broadcasted_iota(jnp.int32, (1, SLOTS), 1) < count, 0.0, LOW)
-    for part in range(2):
-        busy = alive & (part * 2 * QBLOCK < count)
-
-        @pl.when(busy)
-        def _():
-            for block in range(part * 2, part * 2 + 2):
-                to = pl.ds(block * QBLOCK, QBLOCK)
-                scores = dot(qc[to, :], kc[...], True) + bias
-                top = jnp.max(scores, axis=-1, keepdims=True)
-                expo = jnp.exp2((scores - top) * GAIN).astype(jnp.bfloat16)
-                mixed = dot(expo, vc[...])
-                made[frame, to, column] = (mixed[:, :HEAD] / mixed[:, HEAD:]).astype(jnp.bfloat16)
-
-        @pl.when(jnp.logical_not(busy))
-        def _():
-            made[frame, pl.ds(part * 2 * QBLOCK, 2 * QBLOCK), column] = jnp.zeros((2 * QBLOCK, HEAD), jnp.bfloat16)
+
+    def attend(block):
+        to = pl.ds(block * QBLOCK, QBLOCK)
+        scores = dot(qc[to, :], kc[...], True) + bias
+        top = jnp.max(scores, axis=-1, keepdims=True)
+        expo = jnp.exp2((scores - top) * GAIN).astype(jnp.bfloat16)
+        mixed = dot(expo, vc[...])
+        made[frame, to, column] = (mixed[:, :HEAD] / mixed[:, HEAD:]).astype(jnp.bfloat16)
+
+    def blank(block):
+        made[frame, pl.ds(block * QBLOCK, QBLOCK), column] = jnp.zeros((QBLOCK, HEAD), jnp.bfloat16)
+
+    @pl.when(alive & (count > QBLOCK))
+    def _():
+        attend(0)
+        attend(1)
+
+    @pl.when(alive & (count <= QBLOCK))
+    def _():
+        attend(0)
+        blank(1)
+
+    @pl.when(jnp.logical_not(alive))
+    def _():
+        blank(0)
+        blank(1)
 
     @pl.when((frame == 1) & (which == CHIPS * number - 1))
     def _():
@@ -394,66 +404,65 @@
     return own, gifts
 
 
-def time_kernel(parts, info, *refs):
-    turned, (vs, outs) = refs[: len(parts)], refs[len(parts) :]
+def time_kernel(at, each_core, info, turned, vs, *refs):
+    outs = refs[-1]
+    rows = outs.shape[2]
     core = (info[ME] >> 1) & 1
+    first = info[START] + at + core * each_core + pl.program_id(1) * (rows // UNIT)
     span = ROW * 2 * UNIT
     down = lax.broadcasted_iota(jnp.int32, (span, span), 0)
     along = lax.broadcasted_iota(jnp.int32, (span, span), 1)
     frame = jnp.where((down & 15) == (along & 15), along >> 4, span)
     ones = jnp.ones((span, HEAD), jnp.bfloat16)
-    done = 0
-    for (at, each_core), ref in zip(parts, turned):
-        first = info[START] + at + core * each_core
-
-        def step(index, carry, ref=ref, first=first, done=done):
-            here = pl.ds(lines(index), UNIT)
-            there = pl.ds(lines(index + done), UNIT)
-            seen = frame < info[FRAMES_OF + first + index]
-            queries = ref[:, 0:2, here, :].reshape(span, HEAD)
-            keys = ref[:, 2:4, here, :].reshape(span, HEAD)
-            values = vs[:, :, there, :].reshape(span, HEAD)
-            scores = jnp.where(seen, dot(queries, keys, True), LOW)
-            top = jnp.max(scores, axis=-1, keepdims=True)
-            expo = jnp.exp2((scores - top) * GAIN).astype(jnp.bfloat16)
-            mixed = dot(expo, jnp.concatenate([values, ones], axis=1))
-            made = (mixed[:, :HEAD] / mixed[:, HEAD:]).astype(jnp.bfloat16)
-            outs[:, :, there, :] = made.reshape(ROW, 2, UNIT, HEAD)
-            return carry
-
-        lax.fori_loop(0, each_core, step, 0, unroll=5 if each_core % 5 == 0 else 1)
-        done += each_core
-
-
-def time_attention(info, turned, values, turn, parts):
+    for index in range(rows // UNIT):
+        here = pl.ds(index * UNIT, UNIT)
+        seen = frame < info[FRAMES_OF + first + index]
+        queries = turned[:, 0:2, here, :].reshape(span, HEAD)
+        keys = turned[:, 2:4, here, :].reshape(span, HEAD)
+        values = vs[:, :, here, :].reshape(span, HEAD)
+        scores = jnp.where(seen, dot(queries, keys, True), LOW)
+        top = jnp.max(scores, axis=-1, keepdims=True)
+        expo = jnp.exp2((scores - top) * GAIN).astype(jnp.bfloat16)
+        mixed = dot(expo, jnp.concatenate([values, ones], axis=1))
+        made = (mixed[:, :HEAD] / mixed[:, HEAD:]).astype(jnp.bfloat16)
+        outs[:, :, here, :] = made.reshape(ROW, 2, UNIT, HEAD)
+
+
+def time_attention(info, turned, values, out, turn, part, done):
     first, number = turn
-    rows = values.shape[2]
-    wide = [pl.BlockSpec((ROW, 4, each * UNIT, HEAD), lambda h: (0, 0, 0, first + h)) for _, each in parts]
-    thin = pl.BlockSpec((ROW, 2, rows, HEAD), lambda h: (0, 0, 0, h))
+    at, each_core = part
+    units = min(each_core, ALONE // 2)
+    rows = units * UNIT
+    wide = pl.BlockSpec((ROW, 4, rows, HEAD), lambda h, i: (0, 0, i, first + h))
+    thin = pl.BlockSpec((ROW, 2, rows, HEAD), lambda h, i: (0, 0, done // units + i, h))
+    made = pl.BlockSpec((ROW, 2, rows, HEAD), lambda h, i: (0, 0, i, first + h))
     return pl.pallas_call(
-        partial(time_kernel, parts),
-        grid=(number,),
-        in_specs=[SMEM, *wide, thin],
-        out_specs=thin,
-        out_shape=half(ROW, 2, rows, number * HEAD),
+        partial(time_kernel, at, each_core),
+        grid=(number, each_core // units),
+        in_specs=[SMEM, wide, thin] + ([] if out is None else [ANYWHERE]),
+        out_specs=made,
+        out_shape=half(ROW, 2, each_core * UNIT, PER * HEAD),
+        input_output_aliases={} if out is None else {3: 0},
         compiler_params=params(),
-        cost_estimate=cost(number * rows * 16 * 256 * 128 * 4, number * 5, number * rows * 16 * 256),
+        cost_estimate=cost(number * each_core * 16 * 16 * 256 * 128 * 4, number * 3, number * each_core * 65536),
         name="time",
-    )(info, *turned, values)
+    )(info, turned, values, *([] if out is None else [out]))
 
 
 def divide_kernel(parts, info, pieces, own, *refs):
     gifts, (merged, in_sems, own_sem, gift_sems) = refs[:4], refs[4:]
     columns = pieces.shape[3]
     size = merged.shape[1] // UNIT
-    start = info[START]
+    begin = parts[0][0]
+    start = info[START] + begin
     copies = []
     for place in range(ROW):
         chip, core = chip_and_core(place)
         done = 0
         for index, (at, each_core) in enumerate(parts):
             rows = each_core * UNIT
-            part = merged.at[:, pl.ds(at * UNIT + core * rows, rows), pl.ds(chip * columns, columns)]
+            to = pl.ds((at - begin) * UNIT + core * rows, rows)
+            part = merged.at[:, to, pl.ds(chip * columns, columns)]
             copies.append(
                 pltpu.make_async_copy(pieces.at[place, :, pl.ds(done, rows)], part, in_sems.at[place, index])
             )
@@ -503,33 +512,33 @@
 SOURCE = 80
 
 
-def unpack_kernel(turn, adding, info, own, *refs):
-    gifts, (old, out, held, made, own_sems, gift_sems, out_sems) = refs[:4], refs[4:]
-    first, number = turn
+def unpack_kernel(adding, info, own, *refs):
+    gifts, (other, out, held, made, own_sems, gift_sems, out_sems) = refs[:4], refs[4:]
     me, width, height = info[ME], info[WIDTH], info[HEIGHT]
-    start, kept = info[START], info[KEPT]
+    kept = info[KEPT]
     size = own.shape[1] // UNIT
-
-    def column(ref, frame, chip):
-        return ref.at[frame, :, pl.ds((chip * PER + first) * HEAD, number * HEAD)]
-
-    def place(frame, chip):
-        return made.at[frame, :, pl.ds(chip * number * HEAD, number * HEAD)]
-
-    spots = [(frame, chip) for frame in range(2) for chip in range(CHIPS)]
+    start = info[START] if adding else ALONE
     if adding:
-        all_of([pltpu.make_async_copy(column(old, *spot), place(*spot), out_sems.at[spot]) for spot in spots])
+        all_of([pltpu.make_async_copy(other, made, own_sems.at[0])])
         held[...] = jnp.zeros(held.shape, jnp.bfloat16)
     else:
-        copy = pltpu.make_async_copy(own, held.at[:, pl.ds(0, size * UNIT)], own_sems.at[0])
-        copy.start()
-        held[:, size * UNIT :, :] = jnp.zeros((2, held.shape[1] - size * UNIT, held.shape[2]), jnp.bfloat16)
-        copy.wait()
-        for block in range(size):
+        end = ALONE + size
+        copies = [pltpu.make_async_copy(own, held.at[:, pl.ds(ALONE * UNIT, size * UNIT)], own_sems.at[ROW])]
+        for place in range(ROW):
+            chip, core = chip_and_core(place)
+            rows, columns = other.shape[2], other.shape[3]
+            to = held.at[:, pl.ds(core * rows, rows), pl.ds(chip * columns, columns)]
+            copies.append(pltpu.make_async_copy(other.at[place], to, own_sems.at[place]))
+        for copy in copies:
+            copy.start()
+        held[:, end * UNIT :, :] = jnp.zeros((2, held.shape[1] - end * UNIT, FEATURES), jnp.bfloat16)
+        for copy in copies:
+            copy.wait()
+        for block in range(ALONE, end):
 
             @pl.when(block >= kept)
             def _():
-                held[:, pl.ds(block * UNIT, UNIT), :] = jnp.zeros((2, UNIT, held.shape[2]), jnp.bfloat16)
+                held[:, pl.ds(block * UNIT, UNIT), :] = jnp.zeros((2, UNIT, FEATURES), jnp.bfloat16)
 
     def each(act):
         if adding:
@@ -552,6 +561,7 @@
 
     each(lambda copy: copy.start())
     each(lambda copy: copy.wait())
+    copies = []
     for index in range(SLOTS // SPREAD):
         row = index * 2
         from_row = pl.multiple_of((row * width) & -16, 16)
@@ -568,36 +578,31 @@
             if adding:
                 value = value + made[frame, to, :].astype(jnp.float32)
             made[frame, to, :] = value.astype(jnp.bfloat16)
-    all_of([pltpu.make_async_copy(place(*spot), column(out, *spot), out_sems.at[spot]) for spot in spots])
-
-
-def unpack(info, own, gifts, out, turn, adding):
-    features = own.shape[2]
-    first = out is None
-
-    def body(info, own, *refs):
-        refs = list(refs)
-        if first:
-            refs.insert(4, None)
-        unpack_kernel(turn, adding, info, own, *refs)
-
+            copy = pltpu.make_async_copy(made.at[frame, to], out.at[frame, to], out_sems.at[frame, index])
+            copy.start()
+            copies.append(copy)
+    for copy in copies:
+        copy.wait()
+
+
+def unpack(info, own, gifts, other, adding):
     return pl.pallas_call(
-        body,
-        in_specs=[SMEM] + [ANYWHERE] * (5 if first else 6),
+        partial(unpack_kernel, adding),
+        in_specs=[SMEM] + [ANYWHERE] * 6,
         out_specs=ANYWHERE,
         out_shape=half(2, SLOTS, FEATURES),
-        input_output_aliases={} if first else {6: 0},
+        input_output_aliases={6: 0} if adding else {},
         scratch_shapes=[
-            pltpu.VMEM((2, SLOTS + SPARE, features), jnp.bfloat16),
-            pltpu.VMEM((2, SLOTS, features), jnp.bfloat16),
-            pltpu.SemaphoreType.DMA((MORE,)),
+            pltpu.VMEM((2, SLOTS + SPARE, FEATURES), jnp.bfloat16),
+            pltpu.VMEM((2, SLOTS, FEATURES), jnp.bfloat16),
+            pltpu.SemaphoreType.DMA((max(MORE, ROW + 1),)),
             pltpu.SemaphoreType.DMA((4, MOST)),
-            pltpu.SemaphoreType.DMA((2, CHIPS)),
+            pltpu.SemaphoreType.DMA((2, SLOTS // SPREAD)),
         ],
         compiler_params=params(),
-        cost_estimate=cost(0, max(1, 12 * features // FEATURES)),
+        cost_estimate=cost(0, 16),
         name="unpack",
-    )(info, own, *gifts, *([] if first else [out]))
+    )(info, own, *gifts, other)
 
 
 def step_along(value, way):
@@ -630,38 +635,42 @@
     head = exchange(alone)
     gifts = give(gifts)
     spaced = []
+    merged = []
     late = after(info, own)
     for index, turn in enumerate(TURNS):
         made, sent = space(late, query_space, key_space, value_space, turn)
-        spaced.append((made, give(sent)))
+        sent = give(sent)
+        spaced.append((made, sent))
         if index == 0:
             pieces = merge(info, own, after(gifts, made), MAIN[1:])
-            late = after(info, pieces)
             tail = exchange(after(pieces, head))
-    turned = (head, tail)
+            sent = after(sent, pieces)
+        merged.append(merge(info, made, sent, MAIN))
+        late = after(info, pieces, merged[-1])
     previous = tail
     values = []
-    for index, (made, sent) in enumerate(spaced):
-        if index + 1 < len(spaced):
-            sent = after(sent, spaced[index + 1][0])
-        previous = exchange(after(merge(info, made, sent, MAIN), previous))
+    for pieces in merged:
+        previous = exchange(after(pieces, previous, spaced[-1][0]))
         values.append(previous)
-    out = None
-    for index, turn in enumerate(TURNS):
-        made = time_attention(info, turned, values[index], turn, MAIN)
-        previous = exchange(after(made, previous))
-        mine, back = divide(info, previous if out is None else after(previous, out), MAIN)
-        out = unpack(info, mine, give_back(back), out, turn, False)
+    made_head = made_tail = None
+    for turn, value in zip(TURNS, values):
+        made_tail = time_attention(info, tail, value, made_tail, turn, MAIN[1], ALONE // 2)
+        if turn is TURNS[-1]:
+            back_tail = exchange(made_tail)
+        made_head = time_attention(info, head, value, made_head, turn, MAIN[0], 0)
+    back_head = exchange(after(made_head, back_tail))
+    mine, back = divide(info, back_tail, MAIN[1:])
+    out = unpack(info, mine, give_back(back), back_head, False)
 
     def further(index, out):
         here = info.at[START].set(ALONE + REST + index * MORE)
-        turned = (exchange(merge(here, own, gifts, FURTHER)),)
-        for (made, sent), turn in zip(spaced, TURNS):
-            values = exchange(merge(here, made, sent, FURTHER))
-            back = exchange(time_attention(here, turned, values, turn, FURTHER))
-            mine, back = divide(here, back, FURTHER)
-            out = unpack(here, mine, give_back(back), out, turn, True)
-        return out
+        turned = exchange(merge(here, own, gifts, FURTHER))
+        made = None
+        for (space_made, sent), turn in zip(spaced, TURNS):
+            value = exchange(merge(here, space_made, sent, FURTHER))
+            made = time_attention(here, turned, value, made, turn, FURTHER[0], 0)
+        mine, back = divide(here, exchange(made), FURTHER)
+        return unpack(here, mine, give_back(back), out, True)
 
     return lax.fori_loop(0, passes[0], further, out)
 

time: 258 us -> 236 us (0.915)
  Pallas kernels: 120 us -> 92.9 us
  waiting for transfers between devices: 67.4 us -> 79.8 us
  starting transfers between devices: 61.2 us -> 56.6 us
    pallas_call x2, Pallas kernels: 65.4 us -> 45.7 us  [space(): pl.pallas_call(partial(space_kernel, number), grid=(2, CHIPS * number), i...]
    ppermute x20 -> x16, waiting for transfers between devices: 19.9 us -> 39.3 us  [step_along(): lax.ppermute(value, AXES, [(i, neighbour(i // ROW, way) * ROW + i % ROW)...]
    all_to_all x6, waiting for transfers between devices: 47.4 us -> 40.5 us  [exchange(): lax.all_to_all(pieces, AXES, 0, 0, axis_index_groups=groups, tiled=True)]
    ppermute x20 -> x16, starting transfers between devices: 29.1 us -> 25 us  [step_along(): lax.ppermute(value, AXES, [(i, neighbour(i // ROW, way) * ROW + i % ROW)...]
    pallas_call x2 -> x1, Pallas kernels: 7.07 us -> 3.91 us  [divide(): pl.pallas_call(partial(divide_kernel, parts), in_specs=[SMEM, ANYWHERE],...]
    pallas_call x4 -> x5, Pallas kernels: 22.6 us -> 20.3 us  [the longest x4 14.8 us: time_attention(): pl.pallas_call(partial(time_kernel, at, each_core), grid=(number, each_co...]
    unnamed x30 -> x34, local copies, waits for them, and re-layouts: 5.63 us -> 4.36 us
  transfers between devices with their start and end apart: 26 -> 22, of which waited for: 11 -> 13; matrix products, arithmetic and copies ran while one was open for 0% -> 0% of each run, Pallas kernels for 39% -> 30%
where the time goes in v2:
time: 236 us; the launch traced here: 235 us
  Pallas kernels  92.9 us (39%)
  waiting for transfers between devices  79.8 us (34%)
  starting transfers between devices  56.6 us (24%)
  local copies, waits for them, and re-layouts  4.36 us (2%)
    pallas_call x2, Pallas kernels, space(): pl.pallas_call(partial(space_kernel, number), grid=(2, CHIPS * number), i...  45.7 us
    all_to_all x6, waiting for transfers between devices, exchange(): lax.all_to_all(pieces, AXES, 0, 0, axis_index_groups=groups, tiled=True)  40.5 us
    ppermute x16, waiting for transfers between devices, step_along(): lax.ppermute(value, AXES, [(i, neighbour(i // ROW, way) * ROW + i % ROW)...  39.3 us
    all_to_all x6, starting transfers between devices, exchange(): lax.all_to_all(pieces, AXES, 0, 0, axis_index_groups=groups, tiled=True)  31.6 us
    ppermute x16, starting transfers between devices, step_along(): lax.ppermute(value, AXES, [(i, neighbour(i // ROW, way) * ROW + i % ROW)...  25 us
    pallas_call x4, Pallas kernels, time_attention(): pl.pallas_call(partial(time_kernel, at, each_core), grid=(number, each_co...  14.8 us
    pallas_call x3, Pallas kernels, merge(): pl.pallas_call(partial(merge_kernel, parts), in_specs=[SMEM] + [ANYWHERE]...  11 us
    pallas_call x1, Pallas kernels, pack(): pl.pallas_call(pack_kernel, in_specs=[SMEM, ANYWHERE, ANYWHERE], out_spec...  9.29 us
  transfers between devices with their start and end apart: 22, of which 13 were waited for; matrix products, arithmetic and copies ran while one was open for 0% of the time, Pallas kernels for 30%

profile of v2, /device:TPU:2, one launch (start us, length us, event | category | flops | bytes accessed | tf_op | source)
XLA Modules:
  0.0 234.7 jit_solution(10816211202663106631)
XLA Ops:
  0.0 2.7 %plan.1 = (s32[128]{0:T(128)S(1)}, s32[1]{0:T(128)}) custom-call(s32[1]{0:T(128)} %bitcast.1.place, s32[16]{0:T(128)} %counts.1, s32[16]{0:T(128)} %heights.1, s32[16]{0:T(128)} %widths.1), custom_call_target="tpu_custom_call" | custom-call | flops 1000 | tf_op jit(solution)/shard_map/plan/pallas_call | solution.py:164
  2.7 9.3 %pack.1 = (bf16[4,800,1536]{2,1,0:T(8,128)(2,1)}, bf16[8,4,80,384]{3,2,1,0:T(8,128)(2,1)}, bf16[4,96,1536]{2,1,0:T(8,128)(2,1)}, bf16[4,96,1536]{2,1,0:T(8,128)(...) custom-call(s32[128]{0:T(128)S(1)} %get-tuple-element.350.info, bf16[2,704,1536]{2,1,0:T(8,128)(2,1)} %queries.1, ...), custom_call_target="tpu_custom_call" | custom-call | bytes 41943040 | tf_op jit(solution)/shard_map/pack/pallas_call | solution.py:237
  12.1 5.0 %all-to-all-start.4 = ((bf16[8,4,80,384]{3,2,1,0:T(8,128)(2,1)}), bf16[8,4,80,384]{3,2,1,0:T(8,128)(2,1)}, u32[]{:S(2)}, u32[]{:S(2)}) async-start(bf16[8,4,80,384]{3,2,1,0:T(8,128)(2,1)} %get-tuple-element.340), calls=%async_computation.4 | async-start | bytes 3932160 | tf_op jit(solution)/shard_map/all_to_all | solution.py:624
  17.0 1.9 collective-permute-start.4
  19.0 2.1 collective-permute-start.5
  21.1 1.6 collective-permute-start.6
  22.6 1.7 collective-permute-start.7
  24.3 15.9 %space.2 = (bf16[2,800,512]{2,1,0:T(8,128)(2,1)S(1)}, bf16[2,96,512]{2,1,0:T(8,128)(2,1)}, bf16[2,96,512]{2,1,0:T(8,128)(2,1)}, bf16[2,96,512]{2,1,0:T(8,128)(2,1)}, bf16[2,96,512]{2,1,0:T(8,128)(2,1)}) custom-call(s32[128]{0:T(128)S(1)} %get-tuple-element.350.info, bf16[2,704,1536]{2,1,0:T(8,128)(2,1)} %q_ref.3, bf16[2,704,1536]{2,1,0:T(8,128)(2,1)} %k_ref.3, ...), custom_call_target="tpu_custom_call" | custom-call | flops 4060086272 | bytes 8388608 | tf_op jit(solution)/shard_map/space/pallas_call | solution.py:385
  40.2 7.4 %collective-permute-done.4.refs_0_ = bf16[4,96,1536]{2,1,0:T(8,128)(2,1)S(1)} collective-permute-done((bf16[4,96,1536]{2,1,0:T(8,128)(2,1)}, bf16[4,96,1536]{2,1,0:T(8,128)(2,1)S(1)}, u32[]{:S(2)}, u32[]{:S(2)}) %collective-permute-start.4) | collective-permute-done | bytes 1179680 | tf_op jit(solution)/shard_map/ppermute | solution.py:610
  47.6 0.0 collective-permute-done.5.refs_1_
  47.6 2.7 %collective-permute-done.6.refs_2_ = bf16[4,96,1536]{2,1,0:T(8,128)(2,1)S(1)} collective-permute-done((bf16[4,96,1536]{2,1,0:T(8,128)(2,1)}, bf16[4,96,1536]{2,1,0:T(8,128)(2,1)S(1)}, u32[]{:S(2)}, u32[]{:S(2)}) %collective-permute-start.6) | collective-permute-done | bytes 1179680 | tf_op jit(solution)/shard_map/ppermute | solution.py:610
  50.3 0.0 collective-permute-done.7.refs_3_
  50.3 1.1 copy-done.7
  51.4 0.4 copy-done.8
  51.8 5.3 %merge.18 = bf16[8,4,160,384]{3,2,1,0:T(8,128)(2,1)} custom-call(s32[128]{0:T(128)S(1)} %get-tuple-element.350.info, bf16[4,800,1536]{2,1,0:T(8,128)(2,1)} %get-tuple-element.534.own, bf16[4,96,1536]{2,1,0:T(8,128)(2,1)S(1)} %collective-permute-done.4.refs_0_, bf16[4,96,1536]{2,1,0:T(8,128)(2,1)S(1)} %collective-permute-done.5.refs_1_, ...), custom_call_target="tpu_custom_call" | custom-call | bytes 25165824 | tf_op jit(solution)/shard_map/merge/pallas_call | solution.py:298
  57.2 0.0 all-to-all-done.4.turned
  57.2 4.9 %all-to-all-start.5 = ((bf16[8,4,160,384]{3,2,1,0:T(8,128)(2,1)}), bf16[8,4,160,384]{3,2,1,0:T(8,128)(2,1)}, u32[]{:S(2)}, u32[]{:S(2)}) async-start(bf16[8,4,160,384]{3,2,1,0:T(8,128)(2,1)} %merge.18), calls=%async_computation.5 | async-start | bytes 7864320 | tf_op jit(solution)/shard_map/all_to_all | solution.py:624
  62.1 1.0 collective-permute-start.10
  63.1 2.2 collective-permute-start.11
  65.4 0.0 collective-permute-start.8
  65.4 3.2 %collective-permute-start.9 = (bf16[2,96,512]{2,1,0:T(8,128)(2,1)S(1)}, bf16[2,96,512]{2,1,0:T(8,128)(2,1)S(1)}, u32[]{:S(2)}, u32[]{:S(2)}) collective-permute-start(bf16[2,96,512]{2,1,0:T(8,128)(2,1)S(1)} %copy-done.29), channel_id=1, source_target_pairs={{0,96},{1,97},{2,98},{3,99},{4,100},{5,101},{6,102},{7,103},{8,104... | collective-permute-start | bytes 589832 | tf_op jit(solution)/shard_map/ppermute | solution.py:610
  68.6 1.7 collective-permute-done.10.refs_2_
  70.3 0.0 collective-permute-done.11.refs_3_
  70.3 2.7 %collective-permute-done.8.refs_0_ = bf16[2,96,512]{2,1,0:T(8,128)(2,1)S(1)} collective-permute-done((bf16[2,96,512]{2,1,0:T(8,128)(2,1)S(1)}, bf16[2,96,512]{2,1,0:T(8,128)(2,1)S(1)}, u32[]{:S(2)}, u32[]{:S(2)}) %collective-permute-start.8) | collective-permute-done | bytes 196640 | tf_op jit(solution)/shard_map/ppermute | solution.py:610
  73.0 0.0 collective-permute-done.9.refs_1_
  73.0 0.7 copy-done.25
  73.7 0.7 copy-done.26
  74.3 2.7 %merge.19 = bf16[8,2,240,128]{3,2,1,0:T(8,128)(2,1)} custom-call(s32[128]{0:T(128)S(1)} %get-tuple-element.350.info, bf16[2,800,512]{2,1,0:T(8,128)(2,1)S(1)} %get-tuple-element.544.own, bf16[2,96,512]{2,1,0:T(8,128)(2,1)S(1)} %collective-permute-done.8.refs_0_, bf16[2,96,512]{2,1,0:T(8,128)(2,1)S(1)} %collective-permute-done.9.refs_1_, ...), custom_call_target="tpu_custom_call" | custom-call | bytes 4194304 | tf_op jit(solution)/shard_map/merge/pallas_call | solution.py:298
  77.1 29.8 %space.3 = (bf16[2,800,1024]{2,1,0:T(8,128)(2,1)S(1)}, bf16[2,96,1024]{2,1,0:T(8,128)(2,1)}, bf16[2,96,1024]{2,1,0:T(8,128)(2,1)}, bf16[2,96,1024]{2,1,0:T(8,128)(2,1)}, bf16[2,96,1024]{2,1,0:T(8,128)(2,1)}) custom-call(s32[128]{0:T(128)S(1)} %get-tuple-element.350.info, bf16[2,704,1536]{2,1,0:T(8,128)(2,1)} %q_ref.3, bf16[2,704,1536]{2,1,0:T(8,128)(2,1)} %k_ref.3, ...), custom_call_target="tpu_custom_call" | custom-call | flops 8120172544 | bytes 16777216 | tf_op jit(solution)/shard_map/space/pallas_call | solution.py:385
  106.9 0.8 all-to-all-done.5.turned
  107.7 5.6 %all-to-all-start.6 = ((bf16[8,2,240,128]{3,2,1,0:T(8,128)(2,1)}), bf16[8,2,240,128]{3,2,1,0:T(8,128)(2,1)}, u32[]{:S(2)}, u32[]{:S(2)}) async-start(bf16[8,2,240,128]{3,2,1,0:T(8,128)(2,1)} %merge.19), calls=%async_computation.6 | async-start | bytes 1966080 | tf_op jit(solution)/shard_map/all_to_all | solution.py:624
  113.3 0.0 collective-permute-start.12
  113.3 3.2 %collective-permute-start.13 = (bf16[2,96,1024]{2,1,0:T(8,128)(2,1)}, bf16[2,96,1024]{2,1,0:T(8,128)(2,1)S(1)}, u32[]{:S(2)}, u32[]{:S(2)}) collective-permute-start(bf16[2,96,1024]{2,1,0:T(8,128)(2,1)} %get-tuple-element.353), channel_id=1, source_target_pairs={{0,96},{1,97},{2,98},{3,99},{4,100},{5,101},{6,102},{7,103},{8,104... | collective-permute-start | bytes 1179656 | tf_op jit(solution)/shard_map/ppermute | solution.py:610
  116.5 1.0 collective-permute-start.14
  117.5 2.2 collective-permute-start.15
  119.7 6.1 %collective-permute-done.12.refs_0_ = bf16[2,96,1024]{2,1,0:T(8,128)(2,1)S(1)} collective-permute-done((bf16[2,96,1024]{2,1,0:T(8,128)(2,1)}, bf16[2,96,1024]{2,1,0:T(8,128)(2,1)S(1)}, u32[]{:S(2)}, u32[]{:S(2)}) %collective-permute-start.12) | collective-permute-done | bytes 393248 | tf_op jit(solution)/shard_map/ppermute | solution.py:610
  125.8 0.0 collective-permute-done.13.refs_1_
  125.9 2.7 %collective-permute-done.14.refs_2_ = bf16[2,96,1024]{2,1,0:T(8,128)(2,1)S(1)} collective-permute-done((bf16[2,96,1024]{2,1,0:T(8,128)(2,1)}, bf16[2,96,1024]{2,1,0:T(8,128)(2,1)S(1)}, u32[]{:S(2)}, u32[]{:S(2)}) %collective-permute-start.14) | collective-permute-done | bytes 393248 | tf_op jit(solution)/shard_map/ppermute | solution.py:610
  128.5 0.0 collective-permute-done.15.refs_3_
  128.5 0.7 copy-done.18
  129.3 0.8 copy-done.20
  130.0 2.9 %merge.20 = bf16[8,2,240,256]{3,2,1,0:T(8,128)(2,1)} custom-call(s32[128]{0:T(128)S(1)} %get-tuple-element.350.info, bf16[2,800,1024]{2,1,0:T(8,128)(2,1)S(1)} %get-tuple-element.539.own, bf16[2,96,1024]{2,1,0:T(8,128)(2,1)S(1)} %collective-permute-done.12.refs_0_, bf16[2,96,1024]{2,1,0:T(8,128)(2,1)S(1)} %collective-permute-done.13.refs_1_, ...), custom_call_target="tpu_custom_call" | custom-call | bytes 8388608 | tf_op jit(solution)/shard_map/merge/pallas_call | solution.py:298
  133.0 0.0 all-to-all-done.6.vs
  133.0 4.8 %all-to-all-start.7 = ((bf16[8,2,240,256]{3,2,1,0:T(8,128)(2,1)}), bf16[8,2,240,256]{3,2,1,0:T(8,128)(2,1)}, u32[]{:S(2)}, u32[]{:S(2)}) async-start(bf16[8,2,240,256]{3,2,1,0:T(8,128)(2,1)} %merge.20), calls=%async_computation.7 | async-start | bytes 3932160 | tf_op jit(solution)/shard_map/all_to_all | solution.py:624
  137.8 3.4 %time.10.refs_0_ = bf16[8,2,160,384]{3,2,1,0:T(8,128)(2,1)} custom-call(s32[128]{0:T(128)S(1)} %get-tuple-element.350.info, bf16[8,4,160,384]{3,2,1,0:T(8,128)(2,1)} %all-to-all-done.5.turned, bf16[8,2,240,128]{3,2,1,0:T(8,128)(2,1)} %all-to-all-done.6.vs), custom_call_target="tpu_custom_call" | custom-call | flops 335544320 | bytes 3145728 | tf_op jit(solution)/shard_map/time/pallas_call | solution.py:439
  141.2 21.1 %all-to-all-done.7.vs = bf16[8,2,240,256]{3,2,1,0:T(8,128)(2,1)} async-done(((bf16[8,2,240,256]{3,2,1,0:T(8,128)(2,1)}), bf16[8,2,240,256]{3,2,1,0:T(8,128)(2,1)}, u32[]{:S(2)}, u32[]{:S(2)}) %all-to-all-start.7) | async-done | bytes 1966112 | tf_op jit(solution)/shard_map/all_to_all | solution.py:624
  162.3 5.5 %time.11 = bf16[8,2,160,384]{3,2,1,0:T(8,128)(2,1)} custom-call(s32[128]{0:T(128)S(1)} %get-tuple-element.350.info, bf16[8,4,160,384]{3,2,1,0:T(8,128)(2,1)} %all-to-all-done.5.turned, bf16[8,2,240,256]{3,2,1,0:T(8,128)(2,1)} %all-to-all-done.7.vs, bf16[8,2,160,384]{3,2,1,0:T(8,128)(2,1)} %time.10.refs_0_), custom_call_target="tpu_custom_call", output_to_operand_aliasing={{}: (3, {})} | custom-call | flops 671088640 | bytes 6291456 | tf_op jit(solution)/shard_map/time/pallas_call | solution.py:439
  167.8 5.7 %all-to-all-start.8 = ((bf16[8,2,160,384]{3,2,1,0:T(8,128)(2,1)}), bf16[8,2,160,384]{3,2,1,0:T(8,128)(2,1)}, u32[]{:S(2)}, u32[]{:S(2)}) async-start(bf16[8,2,160,384]{3,2,1,0:T(8,128)(2,1)} %time.11), calls=%async_computation.8 | async-start | bytes 3932160 | tf_op jit(solution)/shard_map/all_to_all | solution.py:624
  173.5 2.6 %time.12.refs_0_ = bf16[8,2,80,384]{3,2,1,0:T(8,128)(2,1)} custom-call(s32[128]{0:T(128)S(1)} %get-tuple-element.350.info, bf16[8,4,80,384]{3,2,1,0:T(8,128)(2,1)} %all-to-all-done.4.turned, bf16[8,2,240,128]{3,2,1,0:T(8,128)(2,1)} %all-to-all-done.6.vs), custom_call_target="tpu_custom_call" | custom-call | flops 167772160 | bytes 3145728 | tf_op jit(solution)/shard_map/time/pallas_call | solution.py:439
  176.1 3.3 %time.13 = bf16[8,2,80,384]{3,2,1,0:T(8,128)(2,1)} custom-call(s32[128]{0:T(128)S(1)} %get-tuple-element.350.info, bf16[8,4,80,384]{3,2,1,0:T(8,128)(2,1)} %all-to-all-done.4.turned, bf16[8,2,240,256]{3,2,1,0:T(8,128)(2,1)} %all-to-all-done.7.vs, bf16[8,2,80,384]{3,2,1,0:T(8,128)(2,1)} %time.12.refs_0_), custom_call_target="tpu_custom_call", output_to_operand_aliasing={{}: (3, {})} | custom-call | flops 335544320 | bytes 6291456 | tf_op jit(solution)/shard_map/time/pallas_call | solution.py:439
  179.5 18.6 %all-to-all-done.8.pieces = bf16[8,2,160,384]{3,2,1,0:T(8,128)(2,1)} async-done(((bf16[8,2,160,384]{3,2,1,0:T(8,128)(2,1)}), bf16[8,2,160,384]{3,2,1,0:T(8,128)(2,1)}, u32[]{:S(2)}, u32[]{:S(2)}) %all-to-all-start.8) | async-done | bytes 1966112 | tf_op jit(solution)/shard_map/all_to_all | solution.py:624
  198.0 5.6 %all-to-all-start.9 = ((bf16[8,2,80,384]{3,2,1,0:T(8,128)(2,1)}), bf16[8,2,80,384]{3,2,1,0:T(8,128)(2,1)}, u32[]{:S(2)}, u32[]{:S(2)}) async-start(bf16[8,2,80,384]{3,2,1,0:T(8,128)(2,1)} %time.13), calls=%async_computation.9 | async-start | bytes 1966080 | tf_op jit(solution)/shard_map/all_to_all | solution.py:624
  203.6 3.9 %divide.6 = (bf16[2,320,1536]{2,1,0:T(8,128)(2,1)}, bf16[2,96,1536]{2,1,0:T(8,128)(2,1)}, bf16[2,96,1536]{2,1,0:T(8,128)(2,1)}, bf16[2,96,1536]{2,1,0:T(8,128)(2,1)}, bf16[2,96,1536]{2,1,0:T(8,128)(2,1)}) custom-call(s32[128]{0:T(128)S(1)} %get-tuple-element.350.info, bf16[8,2,160,384]{3,2,1,0:T(8,128)(2,1)} %all-to-all-done.8.pieces), custom_call_target="tpu_custom_call" | custom-call | bytes 8388608 | tf_op jit(solution)/shard_map/divide/pallas_call | solution.py:493
  207.5 0.6 collective-permute-start.16
  208.1 1.5 collective-permute-start.17
  209.6 2.6 %collective-permute-start.18 = (bf16[2,96,1536]{2,1,0:T(8,128)(2,1)}, bf16[2,96,1536]{2,1,0:T(8,128)(2,1)}, u32[]{:S(2)}, u32[]{:S(2)}) collective-permute-start(bf16[2,96,1536]{2,1,0:T(8,128)(2,1)} %get-tuple-element.361), channel_id=1, source_target_pairs={{0,24},{1,25},{2,26},{3,27},{4,28},{5,29},{6,30},{7,31},{8,0},{9,1... | collective-permute-start | bytes 1769480 | tf_op jit(solution)/shard_map/ppermute | solution.py:610
  212.3 0.0 collective-permute-start.19
  212.3 11.0 %collective-permute-done.16.refs_0_ = bf16[2,96,1536]{2,1,0:T(8,128)(2,1)} collective-permute-done((bf16[2,96,1536]{2,1,0:T(8,128)(2,1)}, bf16[2,96,1536]{2,1,0:T(8,128)(2,1)}, u32[]{:S(2)}, u32[]{:S(2)}) %collective-permute-start.16) | collective-permute-done | bytes 589856 | tf_op jit(solution)/shard_map/ppermute | solution.py:610
  223.3 1.5 collective-permute-done.17.refs_1_
  224.7 0.2 collective-permute-done.18.refs_2_
  224.9 3.4 %collective-permute-done.19.refs_3_ = bf16[2,96,1536]{2,1,0:T(8,128)(2,1)} collective-permute-done((bf16[2,96,1536]{2,1,0:T(8,128)(2,1)}, bf16[2,96,1536]{2,1,0:T(8,128)(2,1)}, u32[]{:S(2)}, u32[]{:S(2)}) %collective-permute-start.19) | collective-permute-done | bytes 589856 | tf_op jit(solution)/shard_map/ppermute | solution.py:610
  228.3 0.0 all-to-all-done.9.refs_4_
  228.3 5.5 %unpack.6 = bf16[2,704,1536]{2,1,0:T(8,128)(2,1)} custom-call(s32[128]{0:T(128)S(1)} %get-tuple-element.350.info, bf16[2,320,1536]{2,1,0:T(8,128)(2,1)} %get-tuple-element.358.own, bf16[2,96,1536]{2,1,0:T(8,128)(2,1)} %collective-permute-done.16.refs_0_, bf16[2,96,1536]{2,1,0:T(8,128)(2,1)} %collective-permute-done.17.refs_1_, ...), custom_call_target="tpu_custom_call" | custom-call | bytes 16777216 | tf_op jit(solution)/shard_map/unpack/pallas_call | solution.py:589
  233.9 0.6 while.14
  (28 shorter events, 0.1 us)
Async XLA Ops:
  12.0 10.6 %copy-start.28 = (bf16[4,96,1536]{2,1,0:T(8,128)(2,1)S(1)}, bf16[4,96,1536]{2,1,0:T(8,128)(2,1)}, u32[]{:S(2)}) copy-start(bf16[4,96,1536]{2,1,0:T(8,128)(2,1)} %get-tuple-element.333) | copy-start | bytes 3538948
  12.1 45.1 %all-to-all-start.4 = ((bf16[8,4,80,384]{3,2,1,0:T(8,128)(2,1)}), bf16[8,4,80,384]{3,2,1,0:T(8,128)(2,1)}, u32[]{:S(2)}, u32[]{:S(2)}) async-start(bf16[8,4,80,384]{3,2,1,0:T(8,128)(2,1)} %get-tuple-element.340), calls=%async_computation.4 | async-start | bytes 3932160 | tf_op jit(solution)/shard_map/all_to_all | solution.py:624
  17.0 30.5 %collective-permute-start.4 = (bf16[4,96,1536]{2,1,0:T(8,128)(2,1)}, bf16[4,96,1536]{2,1,0:T(8,128)(2,1)S(1)}, u32[]{:S(2)}, u32[]{:S(2)}) collective-permute-start(bf16[4,96,1536]{2,1,0:T(8,128)(2,1)} %get-tuple-element.330), channel_id=1, source_target_pairs={{0,32},{1,33},{2,34},{3,35},{4,36},{5,37},{6,38},{7,39},{8,40},{9,... | collective-permute-start | bytes 3538952 | tf_op jit(solution)/shard_map/ppermute | solution.py:610
  19.0 28.6 %collective-permute-start.5 = (bf16[4,96,1536]{2,1,0:T(8,128)(2,1)}, bf16[4,96,1536]{2,1,0:T(8,128)(2,1)S(1)}, u32[]{:S(2)}, u32[]{:S(2)}) collective-permute-start(bf16[4,96,1536]{2,1,0:T(8,128)(2,1)} %get-tuple-element.331), channel_id=1, source_target_pairs={{0,96},{1,97},{2,98},{3,99},{4,100},{5,101},{6,102},{7,103},{8,104... | collective-permute-start | bytes 3538952 | tf_op jit(solution)/shard_map/ppermute | solution.py:610
  21.1 29.2 %collective-permute-start.6 = (bf16[4,96,1536]{2,1,0:T(8,128)(2,1)}, bf16[4,96,1536]{2,1,0:T(8,128)(2,1)S(1)}, u32[]{:S(2)}, u32[]{:S(2)}) collective-permute-start(bf16[4,96,1536]{2,1,0:T(8,128)(2,1)} %get-tuple-element.332), channel_id=1, source_target_pairs={{0,8},{1,9},{2,10},{3,11},{4,12},{5,13},{6,14},{7,15},{8,16},{9,17... | collective-permute-start | bytes 3538952 | tf_op jit(solution)/shard_map/ppermute | solution.py:610
  22.6 27.7 %collective-permute-start.7 = (bf16[4,96,1536]{2,1,0:T(8,128)(2,1)S(1)}, bf16[4,96,1536]{2,1,0:T(8,128)(2,1)S(1)}, u32[]{:S(2)}, u32[]{:S(2)}) collective-permute-start(bf16[4,96,1536]{2,1,0:T(8,128)(2,1)S(1)} %copy-done.28), channel_id=1, source_target_pairs={{0,24},{1,25},{2,26},{3,27},{4,28},{5,29},{6,30},{7,31},{8,0},{9,1... | collective-permute-start | bytes 3538952 | tf_op jit(solution)/shard_map/ppermute | solution.py:610
  40.2 32.8 %copy-start.3 = (bf16[2,800,512]{2,1,0:T(8,128)(2,1)}, bf16[2,800,512]{2,1,0:T(8,128)(2,1)S(1)}, u32[]{:S(2)}) copy-start(bf16[2,800,512]{2,1,0:T(8,128)(2,1)S(1)} %get-tuple-element.544.own) | copy-start | bytes 4915204
  47.6 2.7 %copy-start.5 = (bf16[4,96,1536]{2,1,0:T(8,128)(2,1)}, bf16[4,96,1536]{2,1,0:T(8,128)(2,1)S(1)}, u32[]{:S(2)}) copy-start(bf16[4,96,1536]{2,1,0:T(8,128)(2,1)S(1)} %collective-permute-done.4.refs_0_) | copy-start | bytes 3538948
  47.6 2.8 %copy-start.6 = (bf16[4,96,1536]{2,1,0:T(8,128)(2,1)}, bf16[4,96,1536]{2,1,0:T(8,128)(2,1)S(1)}, u32[]{:S(2)}) copy-start(bf16[4,96,1536]{2,1,0:T(8,128)(2,1)S(1)} %collective-permute-done.5.refs_1_) | copy-start | bytes 3538948
  50.3 1.1 copy-start.7
  50.3 1.5 copy-start.8
  57.1 5.0 %copy-start.32 = (bf16[2,96,512]{2,1,0:T(8,128)(2,1)S(1)}, bf16[2,96,512]{2,1,0:T(8,128)(2,1)}, u32[]{:S(2)}) copy-start(bf16[2,96,512]{2,1,0:T(8,128)(2,1)} %get-tuple-element.344) | copy-start | bytes 589828
  57.1 6.0 %copy-start.31 = (bf16[2,96,512]{2,1,0:T(8,128)(2,1)S(1)}, bf16[2,96,512]{2,1,0:T(8,128)(2,1)}, u32[]{:S(2)}) copy-start(bf16[2,96,512]{2,1,0:T(8,128)(2,1)} %get-tuple-element.345) | copy-start | bytes 589828
  57.1 8.2 %copy-start.30 = (bf16[2,96,512]{2,1,0:T(8,128)(2,1)S(1)}, bf16[2,96,512]{2,1,0:T(8,128)(2,1)}, u32[]{:S(2)}) copy-start(bf16[2,96,512]{2,1,0:T(8,128)(2,1)} %get-tuple-element.342) | copy-start | bytes 589828
  57.1 8.2 %copy-start.29 = (bf16[2,96,512]{2,1,0:T(8,128)(2,1)S(1)}, bf16[2,96,512]{2,1,0:T(8,128)(2,1)}, u32[]{:S(2)}) copy-start(bf16[2,96,512]{2,1,0:T(8,128)(2,1)} %get-tuple-element.343) | copy-start | bytes 589828
  57.2 50.5 %all-to-all-start.5 = ((bf16[8,4,160,384]{3,2,1,0:T(8,128)(2,1)}), bf16[8,4,160,384]{3,2,1,0:T(8,128)(2,1)}, u32[]{:S(2)}, u32[]{:S(2)}) async-start(bf16[8,4,160,384]{3,2,1,0:T(8,128)(2,1)} %merge.18), calls=%async_computation.5 | async-start | bytes 7864320 | tf_op jit(solution)/shard_map/all_to_all | solution.py:624
  62.1 8.2 %collective-permute-start.10 = (bf16[2,96,512]{2,1,0:T(8,128)(2,1)S(1)}, bf16[2,96,512]{2,1,0:T(8,128)(2,1)S(1)}, u32[]{:S(2)}, u32[]{:S(2)}) collective-permute-start(bf16[2,96,512]{2,1,0:T(8,128)(2,1)S(1)} %copy-done.32), channel_id=1, source_target_pairs={{0,8},{1,9},{2,10},{3,11},{4,12},{5,13},{6,14},{7,15},{8,16},{9,17... | collective-permute-start | bytes 589832 | tf_op jit(solution)/shard_map/ppermute | solution.py:610
  63.1 7.1 %collective-permute-start.11 = (bf16[2,96,512]{2,1,0:T(8,128)(2,1)S(1)}, bf16[2,96,512]{2,1,0:T(8,128)(2,1)S(1)}, u32[]{:S(2)}, u32[]{:S(2)}) collective-permute-start(bf16[2,96,512]{2,1,0:T(8,128)(2,1)S(1)} %copy-done.31), channel_id=1, source_target_pairs={{0,24},{1,25},{2,26},{3,27},{4,28},{5,29},{6,30},{7,31},{8,0},{9,1... | collective-permute-start | bytes 589832 | tf_op jit(solution)/shard_map/ppermute | solution.py:610
  65.4 7.6 %collective-permute-start.8 = (bf16[2,96,512]{2,1,0:T(8,128)(2,1)S(1)}, bf16[2,96,512]{2,1,0:T(8,128)(2,1)S(1)}, u32[]{:S(2)}, u32[]{:S(2)}) collective-permute-start(bf16[2,96,512]{2,1,0:T(8,128)(2,1)S(1)} %copy-done.30), channel_id=1, source_target_pairs={{0,32},{1,33},{2,34},{3,35},{4,36},{5,37},{6,38},{7,39},{8,40},{9,... | collective-permute-start | bytes 589832 | tf_op jit(solution)/shard_map/ppermute | solution.py:610
  65.4 7.6 %collective-permute-start.9 = (bf16[2,96,512]{2,1,0:T(8,128)(2,1)S(1)}, bf16[2,96,512]{2,1,0:T(8,128)(2,1)S(1)}, u32[]{:S(2)}, u32[]{:S(2)}) collective-permute-start(bf16[2,96,512]{2,1,0:T(8,128)(2,1)S(1)} %copy-done.29), channel_id=1, source_target_pairs={{0,96},{1,97},{2,98},{3,99},{4,100},{5,101},{6,102},{7,103},{8,104... | collective-permute-start | bytes 589832 | tf_op jit(solution)/shard_map/ppermute | solution.py:610
  70.3 2.7 %copy-start.24 = (bf16[2,96,512]{2,1,0:T(8,128)(2,1)}, bf16[2,96,512]{2,1,0:T(8,128)(2,1)S(1)}, u32[]{:S(2)}) copy-start(bf16[2,96,512]{2,1,0:T(8,128)(2,1)S(1)} %collective-permute-done.11.refs_3_) | copy-start | bytes 589828
  73.0 0.7 copy-start.25
  73.7 0.7 copy-start.26
  107.7 25.3 %all-to-all-start.6 = ((bf16[8,2,240,128]{3,2,1,0:T(8,128)(2,1)}), bf16[8,2,240,128]{3,2,1,0:T(8,128)(2,1)}, u32[]{:S(2)}, u32[]{:S(2)}) async-start(bf16[8,2,240,128]{3,2,1,0:T(8,128)(2,1)} %merge.19), calls=%async_computation.6 | async-start | bytes 1966080 | tf_op jit(solution)/shard_map/all_to_all | solution.py:624
  113.3 12.6 %collective-permute-start.12 = (bf16[2,96,1024]{2,1,0:T(8,128)(2,1)}, bf16[2,96,1024]{2,1,0:T(8,128)(2,1)S(1)}, u32[]{:S(2)}, u32[]{:S(2)}) collective-permute-start(bf16[2,96,1024]{2,1,0:T(8,128)(2,1)} %get-tuple-element.352), channel_id=1, source_target_pairs={{0,32},{1,33},{2,34},{3,35},{4,36},{5,37},{6,38},{7,39},{8,40},{9,... | collective-permute-start | bytes 1179656 | tf_op jit(solution)/shard_map/ppermute | solution.py:610
  113.3 12.6 %collective-permute-start.13 = (bf16[2,96,1024]{2,1,0:T(8,128)(2,1)}, bf16[2,96,1024]{2,1,0:T(8,128)(2,1)S(1)}, u32[]{:S(2)}, u32[]{:S(2)}) collective-permute-start(bf16[2,96,1024]{2,1,0:T(8,128)(2,1)} %get-tuple-element.353), channel_id=1, source_target_pairs={{0,96},{1,97},{2,98},{3,99},{4,100},{5,101},{6,102},{7,103},{8,104... | collective-permute-start | bytes 1179656 | tf_op jit(solution)/shard_map/ppermute | solution.py:610
  116.5 12.0 %collective-permute-start.14 = (bf16[2,96,1024]{2,1,0:T(8,128)(2,1)}, bf16[2,96,1024]{2,1,0:T(8,128)(2,1)S(1)}, u32[]{:S(2)}, u32[]{:S(2)}) collective-permute-start(bf16[2,96,1024]{2,1,0:T(8,128)(2,1)} %get-tuple-element.354), channel_id=1, source_target_pairs={{0,8},{1,9},{2,10},{3,11},{4,12},{5,13},{6,14},{7,15},{8,16},{9,17... | collective-permute-start | bytes 1179656 | tf_op jit(solution)/shard_map/ppermute | solution.py:610
  117.5 11.0 %collective-permute-start.15 = (bf16[2,96,1024]{2,1,0:T(8,128)(2,1)}, bf16[2,96,1024]{2,1,0:T(8,128)(2,1)S(1)}, u32[]{:S(2)}, u32[]{:S(2)}) collective-permute-start(bf16[2,96,1024]{2,1,0:T(8,128)(2,1)} %get-tuple-element.355), channel_id=1, source_target_pairs={{0,24},{1,25},{2,26},{3,27},{4,28},{5,29},{6,30},{7,31},{8,0},{9,1... | collective-permute-start | bytes 1179656 | tf_op jit(solution)/shard_map/ppermute | solution.py:610
  125.8 2.7 %copy-start.14 = (bf16[2,96,1024]{2,1,0:T(8,128)(2,1)}, bf16[2,96,1024]{2,1,0:T(8,128)(2,1)S(1)}, u32[]{:S(2)}) copy-start(bf16[2,96,1024]{2,1,0:T(8,128)(2,1)S(1)} %collective-permute-done.12.refs_0_) | copy-start | bytes 1179652
  125.9 2.7 %copy-start.16 = (bf16[2,96,1024]{2,1,0:T(8,128)(2,1)}, bf16[2,96,1024]{2,1,0:T(8,128)(2,1)S(1)}, u32[]{:S(2)}) copy-start(bf16[2,96,1024]{2,1,0:T(8,128)(2,1)S(1)} %collective-permute-done.13.refs_1_) | copy-start | bytes 1179652
  128.5 0.8 copy-start.18
  129.3 0.8 copy-start.20
  133.0 29.3 %all-to-all-start.7 = ((bf16[8,2,240,256]{3,2,1,0:T(8,128)(2,1)}), bf16[8,2,240,256]{3,2,1,0:T(8,128)(2,1)}, u32[]{:S(2)}, u32[]{:S(2)}) async-start(bf16[8,2,240,256]{3,2,1,0:T(8,128)(2,1)} %merge.20), calls=%async_computation.7 | async-start | bytes 3932160 | tf_op jit(solution)/shard_map/all_to_all | solution.py:624
  167.8 30.2 %all-to-all-start.8 = ((bf16[8,2,160,384]{3,2,1,0:T(8,128)(2,1)}), bf16[8,2,160,384]{3,2,1,0:T(8,128)(2,1)}, u32[]{:S(2)}, u32[]{:S(2)}) async-start(bf16[8,2,160,384]{3,2,1,0:T(8,128)(2,1)} %time.11), calls=%async_computation.8 | async-start | bytes 3932160 | tf_op jit(solution)/shard_map/all_to_all | solution.py:624
  198.0 30.3 %all-to-all-start.9 = ((bf16[8,2,80,384]{3,2,1,0:T(8,128)(2,1)}), bf16[8,2,80,384]{3,2,1,0:T(8,128)(2,1)}, u32[]{:S(2)}, u32[]{:S(2)}) async-start(bf16[8,2,80,384]{3,2,1,0:T(8,128)(2,1)} %time.13), calls=%async_computation.9 | async-start | bytes 1966080 | tf_op jit(solution)/shard_map/all_to_all | solution.py:624
  207.5 15.8 %collective-permute-start.16 = (bf16[2,96,1536]{2,1,0:T(8,128)(2,1)}, bf16[2,96,1536]{2,1,0:T(8,128)(2,1)}, u32[]{:S(2)}, u32[]{:S(2)}) collective-permute-start(bf16[2,96,1536]{2,1,0:T(8,128)(2,1)} %get-tuple-element.359), channel_id=1, source_target_pairs={{0,96},{1,97},{2,98},{3,99},{4,100},{5,101},{6,102},{7,103},{8,104... | collective-permute-start | bytes 1769480 | tf_op jit(solution)/shard_map/ppermute | solution.py:610
  208.1 16.6 %collective-permute-start.17 = (bf16[2,96,1536]{2,1,0:T(8,128)(2,1)}, bf16[2,96,1536]{2,1,0:T(8,128)(2,1)}, u32[]{:S(2)}, u32[]{:S(2)}) collective-permute-start(bf16[2,96,1536]{2,1,0:T(8,128)(2,1)} %get-tuple-element.360), channel_id=1, source_target_pairs={{0,32},{1,33},{2,34},{3,35},{4,36},{5,37},{6,38},{7,39},{8,40},{9,... | collective-permute-start | bytes 1769480 | tf_op jit(solution)/shard_map/ppermute | solution.py:610
  209.6 15.3 %collective-permute-start.18 = (bf16[2,96,1536]{2,1,0:T(8,128)(2,1)}, bf16[2,96,1536]{2,1,0:T(8,128)(2,1)}, u32[]{:S(2)}, u32[]{:S(2)}) collective-permute-start(bf16[2,96,1536]{2,1,0:T(8,128)(2,1)} %get-tuple-element.361), channel_id=1, source_target_pairs={{0,24},{1,25},{2,26},{3,27},{4,28},{5,29},{6,30},{7,31},{8,0},{9,1... | collective-permute-start | bytes 1769480 | tf_op jit(solution)/shard_map/ppermute | solution.py:610
  212.3 16.1 %collective-permute-start.19 = (bf16[2,96,1536]{2,1,0:T(8,128)(2,1)}, bf16[2,96,1536]{2,1,0:T(8,128)(2,1)}, u32[]{:S(2)}, u32[]{:S(2)}) collective-permute-start(bf16[2,96,1536]{2,1,0:T(8,128)(2,1)} %get-tuple-element.362), channel_id=1, source_target_pairs={{0,8},{1,9},{2,10},{3,11},{4,12},{5,13},{6,14},{7,15},{8,16},{9,17... | collective-permute-start | bytes 1769480 | tf_op jit(solution)/shard_map/ppermute | solution.py:610

commit v3 on v2

--- a/solution.py
+++ b/solution.py
@@ -22,7 +22,7 @@
 LOW = -1e30
 UNIT = 16
 BLOCKS = SLOTS // UNIT
-MOST = 6
+MOST = 5
 SPARE = MOST * UNIT
 DIVISORS = (4, 2, 2)
 ALONE = 10

time: 236 us -> 228 us (0.966)
  Pallas kernels: 92.9 us -> 86.1 us
    pallas_call x2, Pallas kernels: 45.7 us -> 38.2 us  [space(): pl.pallas_call(partial(space_kernel, number), grid=(2, CHIPS * number), i...]
    ppermute x16, waiting for transfers between devices: 39.3 us -> 33 us  [step_along(): lax.ppermute(value, AXES, [(i, neighbour(i // ROW, way) * ROW + i % ROW)...]
    all_to_all x6, waiting for transfers between devices: 40.5 us -> 46.1 us  [exchange(): lax.all_to_all(pieces, AXES, 0, 0, axis_index_groups=groups, tiled=True)]
  transfers between devices with their start and end apart: 22 -> 22, of which waited for: 13 -> 13; matrix products, arithmetic and copies ran while one was open for 0% -> 0% of each run, Pallas kernels for 30% -> 28%
where the time goes in v3:
time: 228 us; the launch traced here: 226 us
  Pallas kernels  86.1 us (38%)
  waiting for transfers between devices  79.1 us (35%)
  starting transfers between devices  55.9 us (25%)
  local copies, waits for them, and re-layouts  4.12 us (2%)
    all_to_all x6, waiting for transfers between devices, exchange(): lax.all_to_all(pieces, AXES, 0, 0, axis_index_groups=groups, tiled=True)  46.1 us
    pallas_call x2, Pallas kernels, space(): pl.pallas_call(partial(space_kernel, number), grid=(2, CHIPS * number), i...  38.2 us
    ppermute x16, waiting for transfers between devices, step_along(): lax.ppermute(value, AXES, [(i, neighbour(i // ROW, way) * ROW + i % ROW)...  33 us
    all_to_all x6, starting transfers between devices, exchange(): lax.all_to_all(pieces, AXES, 0, 0, axis_index_groups=groups, tiled=True)  31.6 us
    ppermute x16, starting transfers between devices, step_along(): lax.ppermute(value, AXES, [(i, neighbour(i // ROW, way) * ROW + i % ROW)...  24.3 us
    pallas_call x4, Pallas kernels, time_attention(): pl.pallas_call(partial(time_kernel, at, each_core), grid=(number, each_co...  14.8 us
    pallas_call x3, Pallas kernels, merge(): pl.pallas_call(partial(merge_kernel, parts), in_specs=[SMEM] + [ANYWHERE]...  11.7 us
    pallas_call x1, Pallas kernels, pack(): pl.pallas_call(pack_kernel, in_specs=[SMEM, ANYWHERE, ANYWHERE], out_spec...  8.98 us
  transfers between devices with their start and end apart: 22, of which 13 were waited for; matrix products, arithmetic and copies ran while one was open for 0% of the time, Pallas kernels for 28%

profile of v3, /device:TPU:2, one launch (start us, length us, event | category | flops | bytes accessed | tf_op | source)
XLA Modules:
  0.0 226.2 jit_solution(6615813830476289837)
XLA Ops:
  0.0 2.8 %plan.1 = (s32[128]{0:T(128)S(1)}, s32[1]{0:T(128)}) custom-call(s32[1]{0:T(128)} %bitcast.1.place, s32[16]{0:T(128)} %counts.1, s32[16]{0:T(128)} %heights.1, s32[16]{0:T(128)} %widths.1), custom_call_target="tpu_custom_call" | custom-call | flops 1000 | tf_op jit(solution)/shard_map/plan/pallas_call | solution.py:164
  2.8 9.0 %pack.1 = (bf16[4,784,1536]{2,1,0:T(8,128)(2,1)}, bf16[8,4,80,384]{3,2,1,0:T(8,128)(2,1)}, bf16[4,80,1536]{2,1,0:T(8,128)(2,1)}, bf16[4,80,1536]{2,1,0:T(8,128)(...) custom-call(s32[128]{0:T(128)S(1)} %get-tuple-element.350.info, bf16[2,704,1536]{2,1,0:T(8,128)(2,1)} %queries.1, ...), custom_call_target="tpu_custom_call" | custom-call | bytes 41943040 | tf_op jit(solution)/shard_map/pack/pallas_call | solution.py:237
  11.8 5.0 %all-to-all-start.4 = ((bf16[8,4,80,384]{3,2,1,0:T(8,128)(2,1)}), bf16[8,4,80,384]{3,2,1,0:T(8,128)(2,1)}, u32[]{:S(2)}, u32[]{:S(2)}) async-start(bf16[8,4,80,384]{3,2,1,0:T(8,128)(2,1)} %get-tuple-element.340), calls=%async_computation.4 | async-start | bytes 3932160 | tf_op jit(solution)/shard_map/all_to_all | solution.py:624
  16.8 1.9 collective-permute-start.4
  18.6 2.1 collective-permute-start.5
  20.8 1.6 collective-permute-start.6
  22.4 1.7 collective-permute-start.7
  24.0 13.2 %space.2 = (bf16[2,784,512]{2,1,0:T(8,128)(2,1)S(1)}, bf16[2,80,512]{2,1,0:T(8,128)(2,1)}, bf16[2,80,512]{2,1,0:T(8,128)(2,1)}, bf16[2,80,512]{2,1,0:T(8,128)(2,1)}, bf16[2,80,512]{2,1,0:T(8,128)(2,1)}) custom-call(s32[128]{0:T(128)S(1)} %get-tuple-element.350.info, bf16[2,704,1536]{2,1,0:T(8,128)(2,1)} %q_ref.3, bf16[2,704,1536]{2,1,0:T(8,128)(2,1)} %k_ref.3, ...), custom_call_target="tpu_custom_call" | custom-call | flops 4060086272 | bytes 8388608 | tf_op jit(solution)/shard_map/space/pallas_call | solution.py:385
  37.3 5.8 %collective-permute-done.4.refs_0_ = bf16[4,80,1536]{2,1,0:T(8,128)(2,1)S(1)} collective-permute-done((bf16[4,80,1536]{2,1,0:T(8,128)(2,1)}, bf16[4,80,1536]{2,1,0:T(8,128)(2,1)S(1)}, u32[]{:S(2)}, u32[]{:S(2)}) %collective-permute-start.4) | collective-permute-done | bytes 983072 | tf_op jit(solution)/shard_map/ppermute | solution.py:610
  43.0 0.0 collective-permute-done.5.refs_1_
  43.0 2.7 %collective-permute-done.6.refs_2_ = bf16[4,80,1536]{2,1,0:T(8,128)(2,1)S(1)} collective-permute-done((bf16[4,80,1536]{2,1,0:T(8,128)(2,1)}, bf16[4,80,1536]{2,1,0:T(8,128)(2,1)S(1)}, u32[]{:S(2)}, u32[]{:S(2)}) %collective-permute-start.6) | collective-permute-done | bytes 983072 | tf_op jit(solution)/shard_map/ppermute | solution.py:610
  45.8 0.0 collective-permute-done.7.refs_3_
  45.8 1.0 copy-done.7
  46.7 0.4 copy-done.8
  47.1 5.8 %merge.18 = bf16[8,4,160,384]{3,2,1,0:T(8,128)(2,1)} custom-call(s32[128]{0:T(128)S(1)} %get-tuple-element.350.info, bf16[4,784,1536]{2,1,0:T(8,128)(2,1)} %get-tuple-element.534.own, bf16[4,80,1536]{2,1,0:T(8,128)(2,1)S(1)} %collective-permute-done.4.refs_0_, bf16[4,80,1536]{2,1,0:T(8,128)(2,1)S(1)} %collective-permute-done.5.refs_1_, ...), custom_call_target="tpu_custom_call" | custom-call | bytes 25165824 | tf_op jit(solution)/shard_map/merge/pallas_call | solution.py:298
  53.0 0.0 all-to-all-done.4.turned
  53.0 4.9 %all-to-all-start.5 = ((bf16[8,4,160,384]{3,2,1,0:T(8,128)(2,1)}), bf16[8,4,160,384]{3,2,1,0:T(8,128)(2,1)}, u32[]{:S(2)}, u32[]{:S(2)}) async-start(bf16[8,4,160,384]{3,2,1,0:T(8,128)(2,1)} %merge.18), calls=%async_computation.5 | async-start | bytes 7864320 | tf_op jit(solution)/shard_map/all_to_all | solution.py:624
  58.0 0.5 collective-permute-start.10
  58.4 2.8 %collective-permute-start.11 = (bf16[2,80,512]{2,1,0:T(8,128)(2,1)S(1)}, bf16[2,80,512]{2,1,0:T(8,128)(2,1)S(1)}, u32[]{:S(2)}, u32[]{:S(2)}) collective-permute-start(bf16[2,80,512]{2,1,0:T(8,128)(2,1)S(1)} %copy-done.28), channel_id=1, source_target_pairs={{0,24},{1,25},{2,26},{3,27},{4,28},{5,29},{6,30},{7,31},{8,0},{9,1... | collective-permute-start | bytes 491528 | tf_op jit(solution)/shard_map/ppermute | solution.py:610
  61.2 0.0 collective-permute-start.8
  61.2 3.2 %collective-permute-start.9 = (bf16[2,80,512]{2,1,0:T(8,128)(2,1)S(1)}, bf16[2,80,512]{2,1,0:T(8,128)(2,1)S(1)}, u32[]{:S(2)}, u32[]{:S(2)}) collective-permute-start(bf16[2,80,512]{2,1,0:T(8,128)(2,1)S(1)} %copy-done.26), channel_id=1, source_target_pairs={{0,96},{1,97},{2,98},{3,99},{4,100},{5,101},{6,102},{7,103},{8,104... | collective-permute-start | bytes 491528 | tf_op jit(solution)/shard_map/ppermute | solution.py:610
  64.5 1.0 collective-permute-done.10.refs_2_
  65.4 0.0 collective-permute-done.11.refs_3_
  65.4 2.7 %collective-permute-done.8.refs_0_ = bf16[2,80,512]{2,1,0:T(8,128)(2,1)S(1)} collective-permute-done((bf16[2,80,512]{2,1,0:T(8,128)(2,1)S(1)}, bf16[2,80,512]{2,1,0:T(8,128)(2,1)S(1)}, u32[]{:S(2)}, u32[]{:S(2)}) %collective-permute-start.8) | collective-permute-done | bytes 163872 | tf_op jit(solution)/shard_map/ppermute | solution.py:610
  68.1 0.0 collective-permute-done.9.refs_1_
  68.1 0.7 copy-done.22
  68.8 0.7 copy-done.23
  69.4 2.7 %merge.19 = bf16[8,2,240,128]{3,2,1,0:T(8,128)(2,1)} custom-call(s32[128]{0:T(128)S(1)} %get-tuple-element.350.info, bf16[2,784,512]{2,1,0:T(8,128)(2,1)S(1)} %get-tuple-element.544.own, bf16[2,80,512]{2,1,0:T(8,128)(2,1)S(1)} %collective-permute-done.8.refs_0_, bf16[2,80,512]{2,1,0:T(8,128)(2,1)S(1)} %collective-permute-done.9.refs_1_, ...), custom_call_target="tpu_custom_call" | custom-call | bytes 4194304 | tf_op jit(solution)/shard_map/merge/pallas_call | solution.py:298
  72.2 24.9 %space.3 = (bf16[2,784,1024]{2,1,0:T(8,128)(2,1)S(1)}, bf16[2,80,1024]{2,1,0:T(8,128)(2,1)}, bf16[2,80,1024]{2,1,0:T(8,128)(2,1)}, bf16[2,80,1024]{2,1,0:T(8,128)(2,1)}, bf16[2,80,1024]{2,1,0:T(8,128)(2,1)}) custom-call(s32[128]{0:T(128)S(1)} %get-tuple-element.350.info, bf16[2,704,1536]{2,1,0:T(8,128)(2,1)} %q_ref.3, bf16[2,704,1536]{2,1,0:T(8,128)(2,1)} %k_ref.3, ...), custom_call_target="tpu_custom_call" | custom-call | flops 8120172544 | bytes 16777216 | tf_op jit(solution)/shard_map/space/pallas_call | solution.py:385
  97.1 6.4 %all-to-all-done.5.turned = bf16[8,4,160,384]{3,2,1,0:T(8,128)(2,1)} async-done(((bf16[8,4,160,384]{3,2,1,0:T(8,128)(2,1)}), bf16[8,4,160,384]{3,2,1,0:T(8,128)(2,1)}, u32[]{:S(2)}, u32[]{:S(2)}) %all-to-all-start.5) | async-done | bytes 3932192 | tf_op jit(solution)/shard_map/all_to_all | solution.py:624
  103.5 5.6 %all-to-all-start.6 = ((bf16[8,2,240,128]{3,2,1,0:T(8,128)(2,1)}), bf16[8,2,240,128]{3,2,1,0:T(8,128)(2,1)}, u32[]{:S(2)}, u32[]{:S(2)}) async-start(bf16[8,2,240,128]{3,2,1,0:T(8,128)(2,1)} %merge.19), calls=%async_computation.6 | async-start | bytes 1966080 | tf_op jit(solution)/shard_map/all_to_all | solution.py:624
  109.1 0.0 collective-permute-start.12
  109.1 3.2 %collective-permute-start.13 = (bf16[2,80,1024]{2,1,0:T(8,128)(2,1)}, bf16[2,80,1024]{2,1,0:T(8,128)(2,1)S(1)}, u32[]{:S(2)}, u32[]{:S(2)}) collective-permute-start(bf16[2,80,1024]{2,1,0:T(8,128)(2,1)} %get-tuple-element.353), channel_id=1, source_target_pairs={{0,96},{1,97},{2,98},{3,99},{4,100},{5,101},{6,102},{7,103},{8,104... | collective-permute-start | bytes 983048 | tf_op jit(solution)/shard_map/ppermute | solution.py:610
  112.3 0.5 collective-permute-start.14
  112.8 2.8 %collective-permute-start.15 = (bf16[2,80,1024]{2,1,0:T(8,128)(2,1)}, bf16[2,80,1024]{2,1,0:T(8,128)(2,1)S(1)}, u32[]{:S(2)}, u32[]{:S(2)}) collective-permute-start(bf16[2,80,1024]{2,1,0:T(8,128)(2,1)} %get-tuple-element.355), channel_id=1, source_target_pairs={{0,24},{1,25},{2,26},{3,27},{4,28},{5,29},{6,30},{7,31},{8,0},{9,1... | collective-permute-start | bytes 983048 | tf_op jit(solution)/shard_map/ppermute | solution.py:610
  115.6 4.7 %collective-permute-done.12.refs_0_ = bf16[2,80,1024]{2,1,0:T(8,128)(2,1)S(1)} collective-permute-done((bf16[2,80,1024]{2,1,0:T(8,128)(2,1)}, bf16[2,80,1024]{2,1,0:T(8,128)(2,1)S(1)}, u32[]{:S(2)}, u32[]{:S(2)}) %collective-permute-start.12) | collective-permute-done | bytes 327712 | tf_op jit(solution)/shard_map/ppermute | solution.py:610
  120.3 0.0 collective-permute-done.13.refs_1_
  120.3 2.7 %collective-permute-done.14.refs_2_ = bf16[2,80,1024]{2,1,0:T(8,128)(2,1)S(1)} collective-permute-done((bf16[2,80,1024]{2,1,0:T(8,128)(2,1)}, bf16[2,80,1024]{2,1,0:T(8,128)(2,1)S(1)}, u32[]{:S(2)}, u32[]{:S(2)}) %collective-permute-start.14) | collective-permute-done | bytes 327712 | tf_op jit(solution)/shard_map/ppermute | solution.py:610
  123.0 0.0 collective-permute-done.15.refs_3_
  123.0 0.7 copy-done.16
  123.7 0.7 copy-done.17
  124.4 3.1 %merge.20 = bf16[8,2,240,256]{3,2,1,0:T(8,128)(2,1)} custom-call(s32[128]{0:T(128)S(1)} %get-tuple-element.350.info, bf16[2,784,1024]{2,1,0:T(8,128)(2,1)S(1)} %get-tuple-element.539.own, bf16[2,80,1024]{2,1,0:T(8,128)(2,1)S(1)} %collective-permute-done.12.refs_0_, bf16[2,80,1024]{2,1,0:T(8,128)(2,1)S(1)} %collective-permute-done.13.refs_1_, ...), custom_call_target="tpu_custom_call" | custom-call | bytes 8388608 | tf_op jit(solution)/shard_map/merge/pallas_call | solution.py:298
  127.5 0.0 all-to-all-done.6.vs
  127.5 4.8 %all-to-all-start.7 = ((bf16[8,2,240,256]{3,2,1,0:T(8,128)(2,1)}), bf16[8,2,240,256]{3,2,1,0:T(8,128)(2,1)}, u32[]{:S(2)}, u32[]{:S(2)}) async-start(bf16[8,2,240,256]{3,2,1,0:T(8,128)(2,1)} %merge.20), calls=%async_computation.7 | async-start | bytes 3932160 | tf_op jit(solution)/shard_map/all_to_all | solution.py:624
  132.4 3.4 %time.10.refs_0_ = bf16[8,2,160,384]{3,2,1,0:T(8,128)(2,1)} custom-call(s32[128]{0:T(128)S(1)} %get-tuple-element.350.info, bf16[8,4,160,384]{3,2,1,0:T(8,128)(2,1)} %all-to-all-done.5.turned, bf16[8,2,240,128]{3,2,1,0:T(8,128)(2,1)} %all-to-all-done.6.vs), custom_call_target="tpu_custom_call" | custom-call | flops 335544320 | bytes 3145728 | tf_op jit(solution)/shard_map/time/pallas_call | solution.py:439
  135.8 21.1 %all-to-all-done.7.vs = bf16[8,2,240,256]{3,2,1,0:T(8,128)(2,1)} async-done(((bf16[8,2,240,256]{3,2,1,0:T(8,128)(2,1)}), bf16[8,2,240,256]{3,2,1,0:T(8,128)(2,1)}, u32[]{:S(2)}, u32[]{:S(2)}) %all-to-all-start.7) | async-done | bytes 1966112 | tf_op jit(solution)/shard_map/all_to_all | solution.py:624
  156.9 5.5 %time.11 = bf16[8,2,160,384]{3,2,1,0:T(8,128)(2,1)} custom-call(s32[128]{0:T(128)S(1)} %get-tuple-element.350.info, bf16[8,4,160,384]{3,2,1,0:T(8,128)(2,1)} %all-to-all-done.5.turned, bf16[8,2,240,256]{3,2,1,0:T(8,128)(2,1)} %all-to-all-done.7.vs, bf16[8,2,160,384]{3,2,1,0:T(8,128)(2,1)} %time.10.refs_0_), custom_call_target="tpu_custom_call", output_to_operand_aliasing={{}: (3, {})} | custom-call | flops 671088640 | bytes 6291456 | tf_op jit(solution)/shard_map/time/pallas_call | solution.py:439
  162.3 5.7 %all-to-all-start.8 = ((bf16[8,2,160,384]{3,2,1,0:T(8,128)(2,1)}), bf16[8,2,160,384]{3,2,1,0:T(8,128)(2,1)}, u32[]{:S(2)}, u32[]{:S(2)}) async-start(bf16[8,2,160,384]{3,2,1,0:T(8,128)(2,1)} %time.11), calls=%async_computation.8 | async-start | bytes 3932160 | tf_op jit(solution)/shard_map/all_to_all | solution.py:624
  168.0 2.6 %time.12.refs_0_ = bf16[8,2,80,384]{3,2,1,0:T(8,128)(2,1)} custom-call(s32[128]{0:T(128)S(1)} %get-tuple-element.350.info, bf16[8,4,80,384]{3,2,1,0:T(8,128)(2,1)} %all-to-all-done.4.turned, bf16[8,2,240,128]{3,2,1,0:T(8,128)(2,1)} %all-to-all-done.6.vs), custom_call_target="tpu_custom_call" | custom-call | flops 167772160 | bytes 3145728 | tf_op jit(solution)/shard_map/time/pallas_call | solution.py:439
  170.6 3.3 %time.13 = bf16[8,2,80,384]{3,2,1,0:T(8,128)(2,1)} custom-call(s32[128]{0:T(128)S(1)} %get-tuple-element.350.info, bf16[8,4,80,384]{3,2,1,0:T(8,128)(2,1)} %all-to-all-done.4.turned, bf16[8,2,240,256]{3,2,1,0:T(8,128)(2,1)} %all-to-all-done.7.vs, bf16[8,2,80,384]{3,2,1,0:T(8,128)(2,1)} %time.12.refs_0_), custom_call_target="tpu_custom_call", output_to_operand_aliasing={{}: (3, {})} | custom-call | flops 335544320 | bytes 6291456 | tf_op jit(solution)/shard_map/time/pallas_call | solution.py:439
  174.0 18.6 %all-to-all-done.8.pieces = bf16[8,2,160,384]{3,2,1,0:T(8,128)(2,1)} async-done(((bf16[8,2,160,384]{3,2,1,0:T(8,128)(2,1)}), bf16[8,2,160,384]{3,2,1,0:T(8,128)(2,1)}, u32[]{:S(2)}, u32[]{:S(2)}) %all-to-all-start.8) | async-done | bytes 1966112 | tf_op jit(solution)/shard_map/all_to_all | solution.py:624
  192.5 5.6 %all-to-all-start.9 = ((bf16[8,2,80,384]{3,2,1,0:T(8,128)(2,1)}), bf16[8,2,80,384]{3,2,1,0:T(8,128)(2,1)}, u32[]{:S(2)}, u32[]{:S(2)}) async-start(bf16[8,2,80,384]{3,2,1,0:T(8,128)(2,1)} %time.13), calls=%async_computation.9 | async-start | bytes 1966080 | tf_op jit(solution)/shard_map/all_to_all | solution.py:624
  198.1 4.1 %divide.6 = (bf16[2,320,1536]{2,1,0:T(8,128)(2,1)}, bf16[2,80,1536]{2,1,0:T(8,128)(2,1)}, bf16[2,80,1536]{2,1,0:T(8,128)(2,1)}, bf16[2,80,1536]{2,1,0:T(8,128)(2,1)}, bf16[2,80,1536]{2,1,0:T(8,128)(2,1)}) custom-call(s32[128]{0:T(128)S(1)} %get-tuple-element.350.info, bf16[8,2,160,384]{3,2,1,0:T(8,128)(2,1)} %all-to-all-done.8.pieces), custom_call_target="tpu_custom_call" | custom-call | bytes 8388608 | tf_op jit(solution)/shard_map/divide/pallas_call | solution.py:493
  202.3 0.1 collective-permute-start.16
  202.3 2.0 collective-permute-start.17
  204.4 1.5 collective-permute-start.18
  205.8 0.6 collective-permute-start.19
  206.4 9.5 %collective-permute-done.16.refs_0_ = bf16[2,80,1536]{2,1,0:T(8,128)(2,1)} collective-permute-done((bf16[2,80,1536]{2,1,0:T(8,128)(2,1)}, bf16[2,80,1536]{2,1,0:T(8,128)(2,1)}, u32[]{:S(2)}, u32[]{:S(2)}) %collective-permute-start.16) | collective-permute-done | bytes 491552 | tf_op jit(solution)/shard_map/ppermute | solution.py:610
  215.9 1.3 collective-permute-done.17.refs_1_
  217.2 0.2 collective-permute-done.18.refs_2_
  217.4 2.4 %collective-permute-done.19.refs_3_ = bf16[2,80,1536]{2,1,0:T(8,128)(2,1)} collective-permute-done((bf16[2,80,1536]{2,1,0:T(8,128)(2,1)}, bf16[2,80,1536]{2,1,0:T(8,128)(2,1)}, u32[]{:S(2)}, u32[]{:S(2)}) %collective-permute-start.19) | collective-permute-done | bytes 491552 | tf_op jit(solution)/shard_map/ppermute | solution.py:610
  219.8 0.0 all-to-all-done.9.refs_4_
  219.8 5.5 %unpack.6 = bf16[2,704,1536]{2,1,0:T(8,128)(2,1)} custom-call(s32[128]{0:T(128)S(1)} %get-tuple-element.350.info, bf16[2,320,1536]{2,1,0:T(8,128)(2,1)} %get-tuple-element.358.own, bf16[2,80,1536]{2,1,0:T(8,128)(2,1)} %collective-permute-done.16.refs_0_, bf16[2,80,1536]{2,1,0:T(8,128)(2,1)} %collective-permute-done.17.refs_1_, ...), custom_call_target="tpu_custom_call" | custom-call | bytes 16777216 | tf_op jit(solution)/shard_map/unpack/pallas_call | solution.py:589
  225.3 0.7 while.14
  (26 shorter events, 0.0 us)
Async XLA Ops:
  11.8 10.6 %copy-start.25 = (bf16[4,80,1536]{2,1,0:T(8,128)(2,1)S(1)}, bf16[4,80,1536]{2,1,0:T(8,128)(2,1)}, u32[]{:S(2)}) copy-start(bf16[4,80,1536]{2,1,0:T(8,128)(2,1)} %get-tuple-element.333) | copy-start | bytes 2949124
  11.8 41.2 %all-to-all-start.4 = ((bf16[8,4,80,384]{3,2,1,0:T(8,128)(2,1)}), bf16[8,4,80,384]{3,2,1,0:T(8,128)(2,1)}, u32[]{:S(2)}, u32[]{:S(2)}) async-start(bf16[8,4,80,384]{3,2,1,0:T(8,128)(2,1)} %get-tuple-element.340), calls=%async_computation.4 | async-start | bytes 3932160 | tf_op jit(solution)/shard_map/all_to_all | solution.py:624
  16.8 26.3 %collective-permute-start.4 = (bf16[4,80,1536]{2,1,0:T(8,128)(2,1)}, bf16[4,80,1536]{2,1,0:T(8,128)(2,1)S(1)}, u32[]{:S(2)}, u32[]{:S(2)}) collective-permute-start(bf16[4,80,1536]{2,1,0:T(8,128)(2,1)} %get-tuple-element.330), channel_id=1, source_target_pairs={{0,32},{1,33},{2,34},{3,35},{4,36},{5,37},{6,38},{7,39},{8,40},{9,... | collective-permute-start | bytes 2949128 | tf_op jit(solution)/shard_map/ppermute | solution.py:610
  18.6 24.4 %collective-permute-start.5 = (bf16[4,80,1536]{2,1,0:T(8,128)(2,1)}, bf16[4,80,1536]{2,1,0:T(8,128)(2,1)S(1)}, u32[]{:S(2)}, u32[]{:S(2)}) collective-permute-start(bf16[4,80,1536]{2,1,0:T(8,128)(2,1)} %get-tuple-element.331), channel_id=1, source_target_pairs={{0,96},{1,97},{2,98},{3,99},{4,100},{5,101},{6,102},{7,103},{8,104... | collective-permute-start | bytes 2949128 | tf_op jit(solution)/shard_map/ppermute | solution.py:610
  20.8 25.0 %collective-permute-start.6 = (bf16[4,80,1536]{2,1,0:T(8,128)(2,1)}, bf16[4,80,1536]{2,1,0:T(8,128)(2,1)S(1)}, u32[]{:S(2)}, u32[]{:S(2)}) collective-permute-start(bf16[4,80,1536]{2,1,0:T(8,128)(2,1)} %get-tuple-element.332), channel_id=1, source_target_pairs={{0,8},{1,9},{2,10},{3,11},{4,12},{5,13},{6,14},{7,15},{8,16},{9,17... | collective-permute-start | bytes 2949128 | tf_op jit(solution)/shard_map/ppermute | solution.py:610
  22.4 23.4 %collective-permute-start.7 = (bf16[4,80,1536]{2,1,0:T(8,128)(2,1)S(1)}, bf16[4,80,1536]{2,1,0:T(8,128)(2,1)S(1)}, u32[]{:S(2)}, u32[]{:S(2)}) collective-permute-start(bf16[4,80,1536]{2,1,0:T(8,128)(2,1)S(1)} %copy-done.25), channel_id=1, source_target_pairs={{0,24},{1,25},{2,26},{3,27},{4,28},{5,29},{6,30},{7,31},{8,0},{9,1... | collective-permute-start | bytes 2949128 | tf_op jit(solution)/shard_map/ppermute | solution.py:610
  37.3 30.9 %copy-start.3 = (bf16[2,784,512]{2,1,0:T(8,128)(2,1)}, bf16[2,784,512]{2,1,0:T(8,128)(2,1)S(1)}, u32[]{:S(2)}) copy-start(bf16[2,784,512]{2,1,0:T(8,128)(2,1)S(1)} %get-tuple-element.544.own) | copy-start | bytes 4816900
  43.0 2.7 %copy-start.5 = (bf16[4,80,1536]{2,1,0:T(8,128)(2,1)}, bf16[4,80,1536]{2,1,0:T(8,128)(2,1)S(1)}, u32[]{:S(2)}) copy-start(bf16[4,80,1536]{2,1,0:T(8,128)(2,1)S(1)} %collective-permute-done.4.refs_0_) | copy-start | bytes 2949124
  43.0 2.7 %copy-start.6 = (bf16[4,80,1536]{2,1,0:T(8,128)(2,1)}, bf16[4,80,1536]{2,1,0:T(8,128)(2,1)S(1)}, u32[]{:S(2)}) copy-start(bf16[4,80,1536]{2,1,0:T(8,128)(2,1)S(1)} %collective-permute-done.5.refs_1_) | copy-start | bytes 2949124
  45.8 1.0 copy-start.7
  45.8 1.3 copy-start.8
  53.0 5.0 %copy-start.29 = (bf16[2,80,512]{2,1,0:T(8,128)(2,1)S(1)}, bf16[2,80,512]{2,1,0:T(8,128)(2,1)}, u32[]{:S(2)}) copy-start(bf16[2,80,512]{2,1,0:T(8,128)(2,1)} %get-tuple-element.344) | copy-start | bytes 491524
  53.0 5.5 %copy-start.28 = (bf16[2,80,512]{2,1,0:T(8,128)(2,1)S(1)}, bf16[2,80,512]{2,1,0:T(8,128)(2,1)}, u32[]{:S(2)}) copy-start(bf16[2,80,512]{2,1,0:T(8,128)(2,1)} %get-tuple-element.345) | copy-start | bytes 491524
  53.0 8.2 %copy-start.27 = (bf16[2,80,512]{2,1,0:T(8,128)(2,1)S(1)}, bf16[2,80,512]{2,1,0:T(8,128)(2,1)}, u32[]{:S(2)}) copy-start(bf16[2,80,512]{2,1,0:T(8,128)(2,1)} %get-tuple-element.342) | copy-start | bytes 491524
  53.0 8.2 %copy-start.26 = (bf16[2,80,512]{2,1,0:T(8,128)(2,1)S(1)}, bf16[2,80,512]{2,1,0:T(8,128)(2,1)}, u32[]{:S(2)}) copy-start(bf16[2,80,512]{2,1,0:T(8,128)(2,1)} %get-tuple-element.343) | copy-start | bytes 491524
  53.0 50.5 %all-to-all-start.5 = ((bf16[8,4,160,384]{3,2,1,0:T(8,128)(2,1)}), bf16[8,4,160,384]{3,2,1,0:T(8,128)(2,1)}, u32[]{:S(2)}, u32[]{:S(2)}) async-start(bf16[8,4,160,384]{3,2,1,0:T(8,128)(2,1)} %merge.18), calls=%async_computation.5 | async-start | bytes 7864320 | tf_op jit(solution)/shard_map/all_to_all | solution.py:624
  58.0 7.5 %collective-permute-start.10 = (bf16[2,80,512]{2,1,0:T(8,128)(2,1)S(1)}, bf16[2,80,512]{2,1,0:T(8,128)(2,1)S(1)}, u32[]{:S(2)}, u32[]{:S(2)}) collective-permute-start(bf16[2,80,512]{2,1,0:T(8,128)(2,1)S(1)} %copy-done.29), channel_id=1, source_target_pairs={{0,8},{1,9},{2,10},{3,11},{4,12},{5,13},{6,14},{7,15},{8,16},{9,17... | collective-permute-start | bytes 491528 | tf_op jit(solution)/shard_map/ppermute | solution.py:610
  58.4 7.0 %collective-permute-start.11 = (bf16[2,80,512]{2,1,0:T(8,128)(2,1)S(1)}, bf16[2,80,512]{2,1,0:T(8,128)(2,1)S(1)}, u32[]{:S(2)}, u32[]{:S(2)}) collective-permute-start(bf16[2,80,512]{2,1,0:T(8,128)(2,1)S(1)} %copy-done.28), channel_id=1, source_target_pairs={{0,24},{1,25},{2,26},{3,27},{4,28},{5,29},{6,30},{7,31},{8,0},{9,1... | collective-permute-start | bytes 491528 | tf_op jit(solution)/shard_map/ppermute | solution.py:610
  61.2 6.9 %collective-permute-start.8 = (bf16[2,80,512]{2,1,0:T(8,128)(2,1)S(1)}, bf16[2,80,512]{2,1,0:T(8,128)(2,1)S(1)}, u32[]{:S(2)}, u32[]{:S(2)}) collective-permute-start(bf16[2,80,512]{2,1,0:T(8,128)(2,1)S(1)} %copy-done.27), channel_id=1, source_target_pairs={{0,32},{1,33},{2,34},{3,35},{4,36},{5,37},{6,38},{7,39},{8,40},{9,... | collective-permute-start | bytes 491528 | tf_op jit(solution)/shard_map/ppermute | solution.py:610
  61.2 6.9 %collective-permute-start.9 = (bf16[2,80,512]{2,1,0:T(8,128)(2,1)S(1)}, bf16[2,80,512]{2,1,0:T(8,128)(2,1)S(1)}, u32[]{:S(2)}, u32[]{:S(2)}) collective-permute-start(bf16[2,80,512]{2,1,0:T(8,128)(2,1)S(1)} %copy-done.26), channel_id=1, source_target_pairs={{0,96},{1,97},{2,98},{3,99},{4,100},{5,101},{6,102},{7,103},{8,104... | collective-permute-start | bytes 491528 | tf_op jit(solution)/shard_map/ppermute | solution.py:610
  68.1 0.7 copy-start.22
  68.8 0.7 copy-start.23
  103.5 24.0 %all-to-all-start.6 = ((bf16[8,2,240,128]{3,2,1,0:T(8,128)(2,1)}), bf16[8,2,240,128]{3,2,1,0:T(8,128)(2,1)}, u32[]{:S(2)}, u32[]{:S(2)}) async-start(bf16[8,2,240,128]{3,2,1,0:T(8,128)(2,1)} %merge.19), calls=%async_computation.6 | async-start | bytes 1966080 | tf_op jit(solution)/shard_map/all_to_all | solution.py:624
  109.1 11.2 %collective-permute-start.12 = (bf16[2,80,1024]{2,1,0:T(8,128)(2,1)}, bf16[2,80,1024]{2,1,0:T(8,128)(2,1)S(1)}, u32[]{:S(2)}, u32[]{:S(2)}) collective-permute-start(bf16[2,80,1024]{2,1,0:T(8,128)(2,1)} %get-tuple-element.352), channel_id=1, source_target_pairs={{0,32},{1,33},{2,34},{3,35},{4,36},{5,37},{6,38},{7,39},{8,40},{9,... | collective-permute-start | bytes 983048 | tf_op jit(solution)/shard_map/ppermute | solution.py:610
  109.1 11.2 %collective-permute-start.13 = (bf16[2,80,1024]{2,1,0:T(8,128)(2,1)}, bf16[2,80,1024]{2,1,0:T(8,128)(2,1)S(1)}, u32[]{:S(2)}, u32[]{:S(2)}) collective-permute-start(bf16[2,80,1024]{2,1,0:T(8,128)(2,1)} %get-tuple-element.353), channel_id=1, source_target_pairs={{0,96},{1,97},{2,98},{3,99},{4,100},{5,101},{6,102},{7,103},{8,104... | collective-permute-start | bytes 983048 | tf_op jit(solution)/shard_map/ppermute | solution.py:610
  112.3 10.6 %collective-permute-start.14 = (bf16[2,80,1024]{2,1,0:T(8,128)(2,1)}, bf16[2,80,1024]{2,1,0:T(8,128)(2,1)S(1)}, u32[]{:S(2)}, u32[]{:S(2)}) collective-permute-start(bf16[2,80,1024]{2,1,0:T(8,128)(2,1)} %get-tuple-element.354), channel_id=1, source_target_pairs={{0,8},{1,9},{2,10},{3,11},{4,12},{5,13},{6,14},{7,15},{8,16},{9,17... | collective-permute-start | bytes 983048 | tf_op jit(solution)/shard_map/ppermute | solution.py:610
  112.8 10.2 %collective-permute-start.15 = (bf16[2,80,1024]{2,1,0:T(8,128)(2,1)}, bf16[2,80,1024]{2,1,0:T(8,128)(2,1)S(1)}, u32[]{:S(2)}, u32[]{:S(2)}) collective-permute-start(bf16[2,80,1024]{2,1,0:T(8,128)(2,1)} %get-tuple-element.355), channel_id=1, source_target_pairs={{0,24},{1,25},{2,26},{3,27},{4,28},{5,29},{6,30},{7,31},{8,0},{9,1... | collective-permute-start | bytes 983048 | tf_op jit(solution)/shard_map/ppermute | solution.py:610
  120.3 2.7 %copy-start.14 = (bf16[2,80,1024]{2,1,0:T(8,128)(2,1)}, bf16[2,80,1024]{2,1,0:T(8,128)(2,1)S(1)}, u32[]{:S(2)}) copy-start(bf16[2,80,1024]{2,1,0:T(8,128)(2,1)S(1)} %collective-permute-done.12.refs_0_) | copy-start | bytes 983044
  120.3 2.7 %copy-start.15 = (bf16[2,80,1024]{2,1,0:T(8,128)(2,1)}, bf16[2,80,1024]{2,1,0:T(8,128)(2,1)S(1)}, u32[]{:S(2)}) copy-start(bf16[2,80,1024]{2,1,0:T(8,128)(2,1)S(1)} %collective-permute-done.13.refs_1_) | copy-start | bytes 983044
  123.0 0.7 copy-start.16
  123.7 0.7 copy-start.17
  127.5 29.3 %all-to-all-start.7 = ((bf16[8,2,240,256]{3,2,1,0:T(8,128)(2,1)}), bf16[8,2,240,256]{3,2,1,0:T(8,128)(2,1)}, u32[]{:S(2)}, u32[]{:S(2)}) async-start(bf16[8,2,240,256]{3,2,1,0:T(8,128)(2,1)} %merge.20), calls=%async_computation.7 | async-start | bytes 3932160 | tf_op jit(solution)/shard_map/all_to_all | solution.py:624
  162.3 30.2 %all-to-all-start.8 = ((bf16[8,2,160,384]{3,2,1,0:T(8,128)(2,1)}), bf16[8,2,160,384]{3,2,1,0:T(8,128)(2,1)}, u32[]{:S(2)}, u32[]{:S(2)}) async-start(bf16[8,2,160,384]{3,2,1,0:T(8,128)(2,1)} %time.11), calls=%async_computation.8 | async-start | bytes 3932160 | tf_op jit(solution)/shard_map/all_to_all | solution.py:624
  192.5 27.2 %all-to-all-start.9 = ((bf16[8,2,80,384]{3,2,1,0:T(8,128)(2,1)}), bf16[8,2,80,384]{3,2,1,0:T(8,128)(2,1)}, u32[]{:S(2)}, u32[]{:S(2)}) async-start(bf16[8,2,80,384]{3,2,1,0:T(8,128)(2,1)} %time.13), calls=%async_computation.9 | async-start | bytes 1966080 | tf_op jit(solution)/shard_map/all_to_all | solution.py:624
  202.3 13.7 %collective-permute-start.16 = (bf16[2,80,1536]{2,1,0:T(8,128)(2,1)}, bf16[2,80,1536]{2,1,0:T(8,128)(2,1)}, u32[]{:S(2)}, u32[]{:S(2)}) collective-permute-start(bf16[2,80,1536]{2,1,0:T(8,128)(2,1)} %get-tuple-element.359), channel_id=1, source_target_pairs={{0,96},{1,97},{2,98},{3,99},{4,100},{5,101},{6,102},{7,103},{8,104... | collective-permute-start | bytes 1474568 | tf_op jit(solution)/shard_map/ppermute | solution.py:610
  202.3 14.9 %collective-permute-start.17 = (bf16[2,80,1536]{2,1,0:T(8,128)(2,1)}, bf16[2,80,1536]{2,1,0:T(8,128)(2,1)}, u32[]{:S(2)}, u32[]{:S(2)}) collective-permute-start(bf16[2,80,1536]{2,1,0:T(8,128)(2,1)} %get-tuple-element.360), channel_id=1, source_target_pairs={{0,32},{1,33},{2,34},{3,35},{4,36},{5,37},{6,38},{7,39},{8,40},{9,... | collective-permute-start | bytes 1474568 | tf_op jit(solution)/shard_map/ppermute | solution.py:610
  204.4 13.0 %collective-permute-start.18 = (bf16[2,80,1536]{2,1,0:T(8,128)(2,1)}, bf16[2,80,1536]{2,1,0:T(8,128)(2,1)}, u32[]{:S(2)}, u32[]{:S(2)}) collective-permute-start(bf16[2,80,1536]{2,1,0:T(8,128)(2,1)} %get-tuple-element.361), channel_id=1, source_target_pairs={{0,24},{1,25},{2,26},{3,27},{4,28},{5,29},{6,30},{7,31},{8,0},{9,1... | collective-permute-start | bytes 1474568 | tf_op jit(solution)/shard_map/ppermute | solution.py:610
  205.8 14.0 %collective-permute-start.19 = (bf16[2,80,1536]{2,1,0:T(8,128)(2,1)}, bf16[2,80,1536]{2,1,0:T(8,128)(2,1)}, u32[]{:S(2)}, u32[]{:S(2)}) collective-permute-start(bf16[2,80,1536]{2,1,0:T(8,128)(2,1)} %get-tuple-element.362), channel_id=1, source_target_pairs={{0,8},{1,9},{2,10},{3,11},{4,12},{5,13},{6,14},{7,15},{8,16},{9,17... | collective-permute-start | bytes 1474568 | tf_op jit(solution)/shard_map/ppermute | solution.py:610
